TPU v7x, 32 devices: a whole 2x2x4 slice. The times are simulated.
32 devices in a mesh: seq: 8 (over z, y), head: 4 (over x, core).
Axes of the slice: x: 2, y: 2, z: 4, core: 2. Of those that a mesh axis runs over, the one named last changes fastest.
Arguments:
- ssd_input: bfloat16 [4096, 128, 128], P('seq', 'head'), may hold values from -3 to 3
- log_decay: float32 [4096, 128], P('seq', 'head'), may hold values from -1.6 to 0, as said below
- input_map: float32 [4096, 8, 128], P('seq', 'head'), may hold values from -0.18 to 0.18
- output_map: float32 [4096, 8, 128], P('seq', 'head'), may hold values from -0.18 to 0.18
- ssd_cotangent: bfloat16 [4096, 128, 128], P('seq', 'head'), may hold values from -3 to 3
- queries: bfloat16 [4096, 8, 128], P('seq', 'head'), may hold values from -100 to 100
- key_rows: bfloat16 [4096, 128], P('seq'), may hold values from -4 to 4
- value_rows: bfloat16 [4096, 128], P('seq'), may hold values from -6 to 6
- attn_cotangent: bfloat16 [4096, 8, 128], P('seq', 'head'), may hold values from -6 to 6
- pair_order: int32 [8], replicated, may hold values from 0 to 7, each once
Outputs:
- grad_input: bfloat16 [4096, 128, 128], P('seq', 'head')
- grad_decay: float32 [4096, 128], P('seq', 'head')
- grad_input_map: float32 [4096, 8, 128], P('seq', 'head')
- grad_output_map: float32 [4096, 8, 128], P('seq', 'head')
- grad_queries: bfloat16 [4096, 8, 128], P('seq', 'head')
- grad_keys: bfloat16 [4096, 128], P('seq')
- grad_values: bfloat16 [4096, 128], P('seq')
Inputs may be any that keep to these rules, and one draw needn't show every extreme that they name: `pair_order`: a permutation of 0 to 7. `log_decay`: negative everywhere.
All inputs are finite; a program needn't handle non-finite values.
Results may differ from a plain program's by a relative error of at most 0.035.
Values may be sent and summed in bfloat16 or wider, within the bound.
A program may use at most 192 MiB of HBM per device.

v0:
```python
import jax
import jax.numpy as jnp
from jax import lax
from jax.sharding import PartitionSpec as P

BLOCK = 128


HIGHEST = lax.Precision.HIGHEST
NEG_FILL = -1e30
TILE_PAIRS = ((0, 0), (1, 0), (1, 1))


def carried_in(array, axis, join, neutral, backward):
    count = lax.axis_size(axis)
    place = lax.axis_index(axis)
    ahead = count - 1 - place if backward else place
    gathered = jax.tree.map(
        lambda a, kind: lax.all_gather(a.astype(kind), axis), array, (jnp.bfloat16, jnp.bfloat16)
    )
    state = jax.tree.map(lambda a, e: jnp.zeros_like(a) + jnp.asarray(e, a.dtype), array, neutral)

    def one(step, state):
        source = count - 1 - step if backward else step
        return join(
            state,
            jax.tree.map(
                lambda a, own: lax.dynamic_index_in_dim(a, source, 0, False).astype(own.dtype),
                gathered,
                array,
            ),
        )

    return lax.fori_loop(0, ahead, one, state)


def through_bf16(values):
    return lax.optimization_barrier(values.astype(jnp.bfloat16)).astype(jnp.float32)


def block_advance(state_now, inputs):
    x_block, a_block, b_block, c_block = inputs
    cumulative = jnp.cumsum(a_block, axis=0)
    block_len = a_block.shape[0]
    causal_mask = (jnp.arange(block_len)[:, None] >= jnp.arange(block_len)[None, :])[
        :, :, None, None
    ]
    decay_grid = jnp.exp(
        jnp.where(causal_mask, cumulative[:, None] - cumulative[None, :], NEG_FILL)
    )
    inner_prod = jnp.einsum("tgn,sgn->tsg", c_block, b_block, precision=HIGHEST)
    weight_grid = (inner_prod[:, :, :, None] * decay_grid).astype(jnp.bfloat16)
    local_part = jnp.einsum(
        "tsge,sgep->tgep", weight_grid, x_block, preferred_element_type=jnp.float32
    )
    c_scaled = (c_block[:, :, None, :] * jnp.exp(cumulative)[..., None]).astype(jnp.bfloat16)
    carried_part = jnp.einsum(
        "tgen,genp->tgep",
        c_scaled,
        state_now.astype(jnp.bfloat16),
        preferred_element_type=jnp.float32,
    )
    block_out = (local_part + carried_part).astype(jnp.bfloat16)
    tail_decay = jnp.exp(cumulative[-1][None] - cumulative)
    b_scaled = (b_block[:, :, None, :] * tail_decay[..., None]).astype(jnp.bfloat16)
    fresh_state = jnp.einsum(
        "tgen,tgep->genp", b_scaled, x_block, preferred_element_type=jnp.float32
    )
    return (jnp.exp(cumulative[-1])[..., None, None] * state_now + fresh_state, block_out)


def blocked(values):
    return values.reshape((values.shape[0] // BLOCK, BLOCK) + values.shape[1:])


def run_blocks(x_seq, a_seq, b_seq, c_seq, state_start):
    state_end, block_outs = lax.scan(
        block_advance, state_start, (blocked(x_seq), blocked(a_seq), blocked(b_seq), blocked(c_seq))
    )
    return (block_outs.reshape(x_seq.shape), state_end)


def local_state(x_local, a_local, b_local):
    cumulative = jnp.cumsum(blocked(a_local), axis=1)
    block_total = cumulative[:, -1]
    tail_decay = jnp.exp(block_total[:, None] - cumulative)
    b_scaled = (blocked(b_local)[:, :, :, None, :] * tail_decay[..., None]).astype(jnp.bfloat16)
    fresh_state = jnp.einsum(
        "ctgen,ctgep->cgenp", b_scaled, blocked(x_local), preferred_element_type=jnp.float32
    )
    own_total = jnp.sum(block_total, axis=0)
    later_decay = own_total[None] - jnp.cumsum(block_total, axis=0)
    return (
        jnp.einsum("cge,cgenp->genp", jnp.exp(later_decay), fresh_state, precision=HIGHEST),
        own_total,
    )


def output_pull(a_local, c_local, dy_local):
    cumulative = jnp.cumsum(blocked(a_local), axis=1)
    block_total = cumulative[:, -1]
    earlier_decay = jnp.cumsum(block_total, axis=0) - block_total
    c_scaled = (blocked(c_local)[:, :, :, None, :] * jnp.exp(cumulative)[..., None]).astype(
        jnp.bfloat16
    )
    pulled = jnp.einsum(
        "ctgen,ctgep->cgenp", c_scaled, blocked(dy_local), preferred_element_type=jnp.float32
    )
    return jnp.einsum(
        "cge,cgenp->genp", jnp.exp(earlier_decay), through_bf16(pulled), precision=HIGHEST
    )


def affine_combine(earlier, later):
    return (earlier[0] + later[0], jnp.exp(later[0])[..., None, None] * earlier[1] + later[1])


def tile_scores(query_part, query_at, key_part, key_at, scale_factor):
    raw_scores = (
        jnp.einsum("hqd,kd->hqk", query_part, key_part, preferred_element_type=jnp.float32)
        * scale_factor
    )
    return jnp.where(key_at[None, None, :] <= query_at[None, :, None], raw_scores, NEG_FILL)


def run_tile(flag, work, fallback, operand):
    if flag is None:
        return work(operand)
    return lax.cond(flag, work, fallback, operand)


def unchanged(stat_pair):
    return stat_pair


def per_device(
    ssd_input,
    log_decay,
    input_map,
    output_map,
    ssd_cotangent,
    queries,
    key_rows,
    value_rows,
    attn_cotangent,
    pair_order,
):
    seq_count = lax.axis_size("seq")
    seq_pos = lax.axis_index("seq")
    tok_rows, head_count, head_width = ssd_input.shape
    group_count = input_map.shape[1]
    per_group = head_count // group_count
    x_local = ssd_input.reshape(tok_rows, group_count, per_group, head_width)
    a_local = log_decay.reshape(tok_rows, group_count, per_group)
    dy_local = ssd_cotangent.reshape(tok_rows, group_count, per_group, head_width)
    own_state, own_total = local_state(x_local, a_local, input_map)
    own_pull = output_pull(a_local, output_map, dy_local)
    zero_state = jnp.zeros_like(own_state)
    zero_total = jnp.zeros_like(own_total)
    state_in = carried_in(
        (own_total, own_state), "seq", affine_combine, (zero_total, zero_state), False
    )[1]
    later_grad = carried_in(
        (own_total, own_pull), "seq", affine_combine, (zero_total, zero_state), True
    )[1]
    primal, pullback = jax.vjp(run_blocks, x_local, a_local, input_map, output_map, state_in)
    gradients = pullback((dy_local, later_grad))
    grad_input = gradients[0].reshape(tok_rows, head_count, head_width)
    grad_decay = gradients[1].reshape(tok_rows, head_count)
    grad_input_map = gradients[2]
    grad_output_map = gradients[3]
    att_rows, heads_here, att_width = queries.shape
    half_rows = att_rows // 2
    scale_factor = att_width ** (-0.5)
    keys_all, values_all = (
        lax.all_gather(key_rows, "seq", axis=0, tiled=True),
        lax.all_gather(value_rows, "seq", axis=0, tiled=True),
    )
    last_block = 2 * seq_count - 1
    own_first = pair_order[seq_pos]
    query_ids = (own_first, last_block - own_first)
    offsets = jnp.arange(half_rows)
    query_heads = queries.transpose(1, 0, 2)
    grad_heads = attn_cotangent.transpose(1, 0, 2)
    query_parts = (query_heads[:, :half_rows], query_heads[:, half_rows:])
    grad_parts = (grad_heads[:, :half_rows], grad_heads[:, half_rows:])
    query_pos = (query_ids[0] * half_rows + offsets, query_ids[1] * half_rows + offsets)

    def tile_needed(pair_index, other_first):
        if pair_index == 0:
            return other_first <= own_first
        if pair_index == 2:
            return other_first >= own_first
        return None

    def key_tiles(device, key_index):
        start_row = device * att_rows + key_index * half_rows
        return (
            lax.dynamic_slice_in_dim(keys_all, start_row, half_rows, 0),
            lax.dynamic_slice_in_dim(values_all, start_row, half_rows, 0),
        )

    def stat_turn(device, stat_pairs):
        other_first = pair_order[device]
        key_ids = (other_first, last_block - other_first)
        updated = list(stat_pairs)
        for pair_index in range(3):
            query_index, key_index = TILE_PAIRS[pair_index]
            key_part, value_part = key_tiles(device, key_index)
            key_at = key_ids[key_index] * half_rows + offsets

            def refresh(stat_pair, query_index=query_index, key_part=key_part, key_at=key_at):
                scores = tile_scores(
                    query_parts[query_index], query_pos[query_index], key_part, key_at, scale_factor
                )
                row_top = jnp.maximum(stat_pair[0], jnp.max(scores, axis=-1))
                row_total = stat_pair[1] * jnp.exp(stat_pair[0] - row_top) + jnp.sum(
                    jnp.exp(scores - row_top[..., None]), axis=-1
                )
                return (row_top, row_total)

            updated[query_index] = run_tile(
                tile_needed(pair_index, other_first), refresh, unchanged, updated[query_index]
            )
        return tuple(updated)

    stat_start = jnp.full((heads_here, half_rows), NEG_FILL, jnp.float32)
    sum_start = jnp.zeros((heads_here, half_rows), jnp.float32)
    row_stats = lax.fori_loop(
        0, seq_count, stat_turn, ((stat_start, sum_start), (stat_start, sum_start))
    )

    def tile_probs(query_index, key_part, key_at):
        scores = tile_scores(
            query_parts[query_index], query_pos[query_index], key_part, key_at, scale_factor
        )
        return (
            jnp.exp(scores - row_stats[query_index][0][..., None])
            / row_stats[query_index][1][..., None]
        )

    def out_turn(device, out_sums):
        other_first = pair_order[device]
        key_ids = (other_first, last_block - other_first)
        updated = list(out_sums)
        for pair_index in range(3):
            query_index, key_index = TILE_PAIRS[pair_index]
            key_part, value_part = key_tiles(device, key_index)
            key_at = key_ids[key_index] * half_rows + offsets

            def add_out(
                out_sum,
                query_index=query_index,
                key_part=key_part,
                value_part=value_part,
                key_at=key_at,
            ):
                prob_b = tile_probs(query_index, key_part, key_at).astype(jnp.bfloat16)
                return out_sum + jnp.einsum(
                    "hqk,kd->hqd", prob_b, value_part, preferred_element_type=jnp.float32
                )

            updated[query_index] = run_tile(
                tile_needed(pair_index, other_first), add_out, unchanged, updated[query_index]
            )
        return tuple(updated)

    out_zero = jnp.zeros((heads_here, half_rows, att_width), jnp.float32)
    out_sums = lax.fori_loop(0, seq_count, out_turn, (out_zero, out_zero))
    row_delta = tuple(
        (
            jnp.sum(
                grad_parts[index_part].astype(jnp.float32)
                * out_sums[index_part].astype(jnp.bfloat16).astype(jnp.float32),
                axis=-1,
            )
            for index_part in range(2)
        )
    )
    key_count = keys_all.shape[0]
    tile_zero = jnp.zeros((half_rows, att_width), jnp.float32)

    def grad_turn(device, grad_state):
        query_grads = list(grad_state[:2])
        other_first = pair_order[device]
        key_ids = (other_first, last_block - other_first)
        key_halves = [tile_zero, tile_zero]
        value_halves = [tile_zero, tile_zero]
        for pair_index in range(3):
            query_index, key_index = TILE_PAIRS[pair_index]
            key_part, value_part = key_tiles(device, key_index)
            key_at = key_ids[key_index] * half_rows + offsets

            def tile_grads(
                key_piece, query_index=query_index, value_part=value_part, key_at=key_at
            ):
                probs = tile_probs(query_index, key_piece, key_at)
                prob_grad = jnp.einsum(
                    "hqd,kd->hqk",
                    grad_parts[query_index],
                    value_part,
                    preferred_element_type=jnp.float32,
                )
                dscore = (probs * (prob_grad - row_delta[query_index][..., None])).astype(
                    jnp.bfloat16
                )
                query_add = (
                    jnp.einsum("hqk,kd->hqd", dscore, key_piece, preferred_element_type=jnp.float32)
                    * scale_factor
                )
                prob_b = probs.astype(jnp.bfloat16)
                key_add = (
                    jnp.einsum(
                        "hqk,hqd->kd",
                        dscore,
                        query_parts[query_index],
                        preferred_element_type=jnp.float32,
                    )
                    * scale_factor
                )
                value_add = jnp.einsum(
                    "hqk,hqd->kd",
                    prob_b,
                    grad_parts[query_index],
                    preferred_element_type=jnp.float32,
                )
                return (query_add, key_add, value_add)

            def tile_skip(key_piece):
                return (out_zero, tile_zero, tile_zero)

            added = run_tile(tile_needed(pair_index, other_first), tile_grads, tile_skip, key_part)
            query_grads[query_index] = query_grads[query_index] + added[0]
            key_halves[key_index] = key_halves[key_index] + added[1]
            value_halves[key_index] = value_halves[key_index] + added[2]
        key_grad_all = lax.dynamic_update_slice_in_dim(
            grad_state[2], jnp.concatenate(key_halves, axis=0), device * att_rows, 0
        )
        value_grad_all = lax.dynamic_update_slice_in_dim(
            grad_state[3], jnp.concatenate(value_halves, axis=0), device * att_rows, 0
        )
        return (query_grads[0], query_grads[1], key_grad_all, value_grad_all)

    full_zero = jnp.zeros((key_count, att_width), jnp.float32)
    grad_start = (out_zero, out_zero, full_zero, full_zero)
    grad_state = lax.fori_loop(0, seq_count, grad_turn, grad_start)
    grad_queries = (
        jnp.concatenate((grad_state[0], grad_state[1]), axis=1)
        .transpose(1, 0, 2)
        .astype(jnp.bfloat16)
    )
    key_part_sum, value_part_sum = (
        lax.psum_scatter(
            grad_state[2].astype(jnp.bfloat16), "seq", scatter_dimension=0, tiled=True
        ).astype(jnp.float32),
        lax.psum_scatter(
            grad_state[3].astype(jnp.bfloat16), "seq", scatter_dimension=0, tiled=True
        ).astype(jnp.float32),
    )
    key_total, value_total = (
        lax.psum(key_part_sum.astype(jnp.bfloat16), "head").astype(jnp.float32),
        lax.psum(value_part_sum.astype(jnp.bfloat16), "head").astype(jnp.float32),
    )
    grad_keys = key_total.astype(jnp.bfloat16)
    grad_values = value_total.astype(jnp.bfloat16)
    return (
        grad_input,
        grad_decay,
        grad_input_map,
        grad_output_map,
        grad_queries,
        grad_keys,
        grad_values,
    )


def solution(mesh):
    return jax.shard_map(
        per_device,
        mesh=mesh,
        in_specs=(
            P("seq", "head", None),
            P("seq", "head"),
            P("seq", "head", None),
            P("seq", "head", None),
            P("seq", "head", None),
            P("seq", "head", None),
            P("seq", None),
            P("seq", None),
            P("seq", "head", None),
            P(),
        ),
        out_specs=(
            P("seq", "head", None),
            P("seq", "head"),
            P("seq", "head", None),
            P("seq", "head", None),
            P("seq", "head", None),
            P("seq", None),
            P("seq", None),
        ),
        check_vma=False,
    )
```

profile of v0, /device:TPU:0, one launch (start us, length us, event | category | flops | bytes accessed | tf_op | source)
XLA Modules:
  0.0 880.4 jit_solution(14241668315889429849)
XLA Ops:
  13.3 39.7 %all-gather.9.cloned.1.call-done = bf16[4096,128]{1,0:T(8,128)(2,1)} async-done(((bf16[512,128]{1,0:T(8,128)(2,1)}), bf16[4096,128]{1,0:T(8,128)(2,1)}) %all-gather.9.cloned.1.call-update) | async-done | bytes 1048592 | tf_op jit(solution)/shard_map/all_gather | solution.py:176
  53.0 53.5 %while.163 = (s32[]{:T(128)}, f32[2,256]{1,0:T(2,128)S(1)}, f32[2,256]{1,0:T(2,128)S(1)}, f32[2,256]{1,0:T(2,128)S(1)}, f32[2,256]{1,0:T(2,128)S(1)}, /*index=5*...) while((s32[]{:T(128)}, f32[2,256]{1,0:T(2,128)S(1)}, ...), condition=%wide.region_33.34_spmd.clone.clone, body=%wide.region_22.33_spmd.clone.clone.sunk | while | flops 102830352 | bytes 4355633 | solution.py:229
  106.6 59.2 %while.164 = (s32[]{:T(128)}, f32[2,256,128]{2,1,0:T(8,128)S(1)}, f32[2,256,128]{2,1,0:T(8,128)S(1)}, s32[8]{0:T(128)}, s32[]{:T(128)}, /*index=5*/bf16[4096,128...) while((s32[]{:T(128)}, f32[2,256,128]{2,1,0:T(8,128)S(1)}, ...), condition=%wide.region_39.40_spmd.clone.clone, body=%wide.region_34.39_spmd.clone.clone.sunk | while | flops 203687168 | bytes 3043877 | solution.py:269
  167.2 90.4 %while.165 = (s32[]{:T(128)}, f32[2,256,128]{2,1,0:T(8,128)S(1)}, f32[2,256,128]{2,1,0:T(8,128)S(1)}, bf16[4096,128]{1,0:T(8,128)(2,1)S(1)}, bf16[4096,128]{1,0:...) while((s32[]{:T(128)}, f32[2,256,128]{2,1,0:T(8,128)S(1)}, ...), condition=%wide.region_47.48_spmd.clone.clone, body=%wide.region_42.47_spmd.clone.clone.sunk | while | flops 507970816 | bytes 13338276 | solution.py:346
  176.0 4.6 conditional.29
  189.1 4.6 conditional.29
  251.9 4.6 conditional.29
  261.6 4.7 fusion.202
  266.3 18.2 %fusion.199 = f32[2,16,1,128,128]{4,2,3,1,0:T(1,128)S(1)} fusion(f32[4,2,16,1,1]{0,3,4,2,1:T(1,128)S(1)} %copy.168, f32[4,2,16,128,128]{4,3,2,1,0:T(8,128)S(1)} %fusion.202), kind=kOutput, calls=%fused_computation.308 | convolution fusion | flops 25165824 | bytes 10486272 | tf_op jit(solution)/shard_map/cge,cgenp->genp/dot_general | solution.py:94
  287.7 4.7 fusion.210
  292.4 14.2 %fusion.208 = f32[2,16,1,128,128]{4,2,3,1,0:T(1,128)S(1)} fusion(f32[4,2,16,1,1]{0,3,4,2,1:T(1,128)S(1)} %copy.165, bf16[4,2,16,128,128]{4,3,2,1,0:T(8,128)(2,1)S(1)} %fusion.210), kind=kOutput, calls=%fused_computation.319 | convolution fusion | flops 25165824 | bytes 6291968 | tf_op jit(solution)/shard_map/cge,cgenp->genp/dot_general | solution.py:109
  307.8 5.9 copy.125
  315.4 45.0 %all-gather.3 = bf16[8,2,16]{2,1,0:T(2,128)(2,1)S(1)} all-gather(bf16[1,2,16]{2,1,0:T(2,128)(2,1)S(1)} %convert_bitcast_fusion), channel_id=2, replica_groups=mesh['seq'=8,'head'=4] {'seq'}, dimensions={0}, use_global_device_ids=true | all-gather | bytes 576 | tf_op jit(solution)/shard_map/all_gather | solution.py:19
  362.5 54.0 %reduce-scatter.5.cloned.1.call-done = bf16[512,128]{1,0:T(8,128)(2,1)} async-done(((bf16[4096,128]{1,0:T(8,128)(2,1)}), bf16[512,128]{1,0:T(8,128)(2,1)}) %reduce-scatter.5.cloned.1.call-update) | async-done | bytes 131088 | tf_op jit(solution)/shard_map/reduce_scatter | solution.py:356
  416.5 126.5 %all-gather.15.cloned.1.call-done = bf16[16,16,128,128]{3,2,1,0:T(8,128)(2,1)} async-done(((bf16[2,16,128,128]{3,2,1,0:T(8,128)(2,1)}), bf16[16,16,128,128]{3,2,1,0:T(8,128)(2,1)}) %all-gather.15.cloned.1.call-update) | async-done | bytes 8388624 | tf_op jit(solution)/shard_map/all_gather | solution.py:19
  548.6 85.9 %while.161 = (s32[]{:T(128)}, f32[2,16,128,128]{3,2,1,0:T(8,128)S(1)}, f32[4,128,128,2,16]{2,4,3,1,0:T(8,128)}, f32[4,128,128,2,1]{1,2,3,4,0:T(8,128)}, bf16[4,1...) while((s32[]{:T(128)}, ...), condition=%wide.region_9.10_spmd.clone, body=%wide.region_7.9_spmd.clone.sunk | while | flops 192946176 | bytes 21753176 | solution.py:77
  634.5 33.6 %all-gather.13.cloned.1.call-done = bf16[16,16,128,128]{3,2,1,0:T(8,128)(2,1)} async-done(((bf16[2,16,128,128]{3,2,1,0:T(8,128)(2,1)}), bf16[16,16,128,128]{3,2,1,0:T(8,128)(2,1)}) %all-gather.13.cloned.1.call-update) | async-done | bytes 8388624 | tf_op jit(solution)/shard_map/all_gather | solution.py:19
  668.4 12.0 %while.159 = (s32[]{:T(128)}, f32[2,16,128,128]{3,2,1,0:T(8,128)S(1)}, s32[]{:T(128)}, bf16[8,2,16]{2,1,0:T(2,128)(2,1)S(1)}, bf16[8,2,16,128,128]{4,3,2,1,0:T(8...) while((s32[]{:T(128)}, f32[2,16,128,128]{3,2,1,0:T(8,128)S(1)}, s32[]{:T(128)}, ...), condition=%wide.region_4.5_spmd, body=%wide.region_3.4_spmd.sunk | while | flops 1572902 | bytes 5243347 | solution.py:34
  685.5 183.2 %while.162 = (s32[]{:T(128)}, f32[2,16,128,128]{3,2,1,0:T(8,128)S(1)}, bf16[4,128,2,16,128]{4,3,2,1,0:T(8,128)(2,1)}, f32[4,128,2,16]{1,0,3,2:T(4,128)}, f32[4,1...) while((s32[]{:T(128)}, ...), condition=%wide.region_21.22_spmd.clone, body=%wide.region_10.21_spmd.clone.sunk | while | flops 921165824 | bytes 56298108 | solution.py:77
  694.2 3.4 copy_dynamic-update-slice_fusion.5
  712.4 4.6 fusion.329
  758.2 4.6 fusion.329
  804.0 4.6 fusion.329
  849.8 4.6 fusion.329
  (837 shorter events, 438.9 us)
Async XLA Ops:
  7.2 45.8 %all-gather.9.cloned.1.call-start = ((), (), s32[]{:S(2)}) async-start(), calls=%async_computation.2 | async-start | bytes 1179648 | tf_op jit(solution)/shard_map/all_gather | solution.py:176
  7.9 98.6 %all-gather.11.cloned.1.call-start = ((), (), s32[]{:S(2)}) async-start(), calls=%async_computation.3 | async-start | bytes 1179648 | tf_op jit(solution)/shard_map/all_gather | solution.py:177
  8.6 353.8 %reduce-scatter.3.cloned.1.call-start = ((), (), s32[]{:S(2)}) async-start(), calls=%async_computation.4 | async-start | bytes 1179648 | tf_op jit(solution)/shard_map/reduce_scatter | solution.py:353
  167.2 91.5 %copy-start.2 = (f32[512,32]{0,1:T(8,128)S(1)}, f32[512,32]{0,1:T(8,128)}, u32[]{:S(2)}) copy-start(f32[512,32]{0,1:T(8,128)} %param.37) | copy-start | bytes 196612
  257.6 1.0 copy-start.1
  258.6 157.8 %reduce-scatter.5.cloned.1.call-start = ((), (), s32[]{:S(2)}) async-start(), calls=%async_computation.5 | async-start | bytes 1179648 | tf_op jit(solution)/shard_map/reduce_scatter | solution.py:356
  259.2 283.8 %all-gather.15.cloned.1.call-start = ((), (), s32[]{:S(2)}) async-start(), calls=%async_computation.7 | async-start | bytes 9437184 | tf_op jit(solution)/shard_map/all_gather | solution.py:19
  285.7 382.4 %all-gather.13.cloned.1.call-start = ((), (), s32[]{:S(2)}) async-start(), calls=%async_computation.6 | async-start | bytes 9437184 | tf_op jit(solution)/shard_map/all_gather | solution.py:19
  307.8 562.4 %all-reduce.5.cloned.1.call-start = ((), (), s32[]{:S(2)}) async-start(), calls=%async_computation.8 | async-start | bytes 524288 | tf_op jit(solution)/shard_map/psum | solution.py:361
  701.3 6.0 copy-start
  747.1 6.0 copy-start
  792.9 6.0 copy-start
  838.7 6.0 copy-start
Sparse Core Ops, SparseCore 0:
  10.1 42.8 all-gather.8
  55.1 38.9 all-gather.10
  258.7 91.5 reduce-scatter.2
  353.9 62.4 reduce-scatter.4
  419.0 123.9 all-gather.14
  545.0 123.1 all-gather.12
  670.5 30.2 all-reduce.4
where the time goes:
time: 895 us; the launch traced here: 880 us
  waiting for transfers between devices  255 us (28%)
  local copies, waits for them, and re-layouts  228 us (25%)
  matrix products  162 us (18%)
  other arithmetic  87.1 us (10%)
  loops' own time  86 us (10%)
  blocking collectives  45 us (5%)
  between operations  15.9 us (2%)
    all_gather x2, waiting for transfers between devices, carried_in(): lax.all_gather(a.astype(kind), axis)  160 us
    dynamic_slice x56, local copies, waits for them, and re-layouts, run_blocks(): lax.scan(block_advance, state_start, (blocked(x_seq), blocked(a_seq), blo...  68.6 us
    reduce_scatter x1, waiting for transfers between devices, per_device(): lax.psum_scatter(grad_state[3].astype(jnp.bfloat16), 'seq', scatter_dimen...  54 us
    dynamic_update_slice x56, local copies, waits for them, and re-layouts, run_blocks(): lax.scan(block_advance, state_start, (blocked(x_seq), blocked(a_seq), blo...  47.1 us
    all_gather x1, blocking collectives, carried_in(): lax.all_gather(a.astype(kind), axis)  45 us
    all_gather x1, waiting for transfers between devices, per_device(): lax.all_gather(key_rows, 'seq', axis=0, tiled=True)  39.7 us
    dynamic_update_slice x16, other arithmetic, run_blocks(): lax.scan(block_advance, state_start, (blocked(x_seq), blocked(a_seq), blo...  34.3 us
    another operation x1, loops' own time, per_device(): grad_state = lax.fori_loop(0, seq_count, grad_turn, grad_start)  26.8 us
  transfers between devices with their start and end apart: 7, of which 4 were waited for; matrix products, arithmetic and copies ran while one was open for 43% of the time, Pallas kernels for 0%

commit v1 on v0

v1 whole, which is shorter than its diff:
```python
import functools
import math

import jax
import jax.numpy as jnp
from jax import lax
from jax.experimental import pallas as pl
from jax.experimental.pallas import tpu as pltpu
from jax.sharding import PartitionSpec as P

BLOCK = 128
HIGHEST = lax.Precision.HIGHEST
NEG_FILL = -1e30
F32 = jnp.float32
BF16 = jnp.bfloat16
VMEM_BYTES = 52 * 1024 * 1024


def dot(a, b):
    return jnp.dot(a, b, preferred_element_type=F32)


def dot_t(a, b):
    return lax.dot_general(a, b, (((1,), (1,)), ((), ())), preferred_element_type=F32)


def dot_hi(a, b):
    return jnp.dot(a, b, preferred_element_type=F32, precision=HIGHEST)


def iota2(shape, dim):
    return lax.broadcasted_iota(jnp.int32, shape, dim)


def lower_ones():
    shape = (BLOCK, BLOCK)
    return (iota2(shape, 0) >= iota2(shape, 1)).astype(F32)


def upper_ones():
    shape = (BLOCK, BLOCK)
    return (iota2(shape, 0) <= iota2(shape, 1)).astype(F32)


def state_kernel(x_ref, dy_ref, a_ref, b_ref, c_ref, s_ref, p_ref, tot_ref, tx, ey):
    rows, heads = a_ref.shape[1:]
    width = x_ref.shape[1] // heads
    lower = lower_ones()
    offset = jnp.zeros((1, heads), F32)
    cums = []
    for k in range(rows // BLOCK):
        cum = dot_hi(lower, a_ref[0, pl.ds(k * BLOCK, BLOCK), :])
        cums.append(cum + offset)
        offset = offset + cum[BLOCK - 1 :, :]
    tot_ref[0] = offset
    for k, cum in enumerate(cums):
        span = pl.ds(k * BLOCK, BLOCK)
        tail = jnp.exp(offset - cum)
        head_decay = jnp.exp(cum)
        for h in range(heads):
            lanes = pl.ds(h * width, width)
            tx[span, lanes] = (x_ref[span, lanes].astype(F32) * tail[:, h : h + 1]).astype(BF16)
            ey[span, lanes] = (
                dy_ref[span, lanes].astype(F32) * head_decay[:, h : h + 1]
            ).astype(BF16)
    b_t = b_ref[...].T.astype(BF16)
    c_t = c_ref[...].T.astype(BF16)
    step = 4 * width
    for at in range(0, heads * width, step):
        lanes = pl.ds(at, step)
        s_ref[0, :, lanes] = dot(b_t, tx[:, lanes]).astype(BF16)
        p_ref[0, :, lanes] = dot(c_t, ey[:, lanes]).astype(BF16)


def scan_kernel(
    x_ref,
    dy_ref,
    a_ref,
    at_ref,
    b_ref,
    c_ref,
    s_in,
    ds_in,
    dx_ref,
    da_ref,
    db_ref,
    dc_ref,
    states,
    tails,
    edy,
    s_now,
    ds_now,
    dgt,
):
    rows, heads = a_ref.shape[1:]
    width = x_ref.shape[1] // heads
    count = rows // BLOCK
    lower = lower_ones()
    upper = upper_ones()
    s_now[...] = s_in[0]
    ds_now[...] = ds_in[0]

    def forward(k, carry):
        span = pl.ds(pl.multiple_of(k * BLOCK, BLOCK), BLOCK)
        cum = dot_hi(lower, a_ref[0, span, :])
        last = cum[BLOCK - 1 :, :]
        tail = jnp.exp(last - cum)
        whole = jnp.exp(last)
        b_t = b_ref[span, :].T.astype(BF16)
        for h in range(heads):
            lanes = pl.ds(h * width, width)
            tails[span, lanes] = (
                x_ref[span, lanes].astype(F32) * tail[:, h : h + 1]
            ).astype(BF16)
        for h in range(heads):
            lanes = pl.ds(h * width, width)
            now = s_now[:, lanes]
            states[k, :, lanes] = now.astype(BF16)
            s_now[:, lanes] = now * whole[:, h : h + 1] + dot(b_t, tails[span, lanes])
        return carry

    lax.fori_loop(0, count, forward, 0)
    causal = iota2((BLOCK, BLOCK), 0) <= iota2((BLOCK, BLOCK), 1)

    def backward(turn, carry):
        k = count - 1 - turn
        span = pl.ds(pl.multiple_of(k * BLOCK, BLOCK), BLOCK)
        cum = dot_hi(lower, a_ref[0, span, :])
        cum_t = dot_hi(at_ref[0, :, span], upper)
        last = cum[BLOCK - 1 :, :]
        tail = jnp.exp(last - cum)
        whole = jnp.exp(last)
        grow = jnp.exp(cum)
        b_wide = b_ref[span, :]
        c_wide = c_ref[span, :]
        b_low = b_wide.astype(BF16)
        c_low = c_wide.astype(BF16)
        c_t = c_wide.T.astype(BF16)
        gt = lax.dot_general(
            b_wide, c_wide, (((1,), (1,)), ((), ())), preferred_element_type=F32, precision=HIGHEST
        )
        dgt[...] = jnp.zeros_like(dgt)
        columns = jnp.zeros((BLOCK, heads), F32)
        row_sums = jnp.zeros((heads, BLOCK), F32)
        totals = jnp.zeros((heads, BLOCK), F32)
        column_at = iota2((BLOCK, heads), 1)
        row_at = iota2((heads, BLOCK), 0)
        db = jnp.zeros((BLOCK, b_wide.shape[1]), F32)
        dc = jnp.zeros((BLOCK, b_wide.shape[1]), F32)
        for h in range(heads):
            lanes = pl.ds(h * width, width)
            x_h = x_ref[span, lanes]
            dy_h = dy_ref[span, lanes]
            tail_x = tails[span, lanes]
            state = states[k, :, lanes]
            ds_wide = ds_now[:, lanes]
            ds_low = ds_wide.astype(BF16)
            decay = jnp.exp(
                jnp.where(causal, cum_t[h : h + 1, :] - cum[:, h : h + 1], NEG_FILL)
            )
            t1 = dot_t(x_h, dy_h) * decay
            dgt[...] += t1
            mt = t1 * gt
            from_state = dot(b_low, ds_low)
            dx = dot((gt * decay).astype(BF16), dy_h) + from_state * tail[:, h : h + 1]
            dx_ref[span, lanes] = dx.astype(BF16)
            edy_h = (dy_h.astype(F32) * grow[:, h : h + 1]).astype(BF16)
            r2 = tail_x.astype(F32) * from_state
            column = jnp.sum(
                edy_h.astype(F32) * dot(c_low, state) - r2 - mt, axis=1, keepdims=True
            )
            columns = jnp.where(column_at == h, column, columns)
            row_sums = jnp.where(row_at == h, jnp.sum(mt, axis=0, keepdims=True), row_sums)
            total = jnp.sum(r2, axis=0, keepdims=True) + whole[:, h : h + 1] * jnp.sum(
                ds_wide * state.astype(F32), axis=0, keepdims=True
            )
            totals = jnp.where(row_at == h, total, totals)
            dc = dc + dot_t(edy_h, state)
            db = db + dot_t(tail_x, ds_low)
            ds_now[:, lanes] = ds_wide * whole[:, h : h + 1] + dot(c_t, edy_h)
        dg = dgt[...]
        db_ref[span, :] = db + dot_hi(dg, c_wide)
        dc_ref[span, :] = dc + dot_hi(dg.T, b_wide)
        total = jnp.sum(totals, axis=1, keepdims=True)
        row_sums = row_sums + jnp.where(iota2((heads, BLOCK), 1) == BLOCK - 1, total, 0.0)
        da_ref[0, span, :] = dot_hi(upper, columns + row_sums.T)
        return carry

    lax.fori_loop(0, count, backward, 0)


def attention_kernel(
    place_ref, own_ref, q_ref, do_ref, kv_ref, dq_ref, dkv_ref, scores, probs, acc
):
    halves, lanes_q, width = q_ref.shape
    half = kv_ref.shape[0] // place_ref.shape[0]
    scale = width ** (-0.5)
    rate = scale * math.log2(math.e)
    acc[...] = jnp.zeros_like(acc)
    visible = iota2((half, lanes_q), 0) <= lax.rem(iota2((half, lanes_q), 1), half)

    def rows_of(j):
        return pl.ds(pl.multiple_of(place_ref[j] * half, half), half)

    def fold(op, tile):
        return op(tile.reshape(half // 8, 8, lanes_q), axis=0)

    for i in range(halves):
        own = own_ref[i]
        q = q_ref[i]
        q_t = q.T

        def score(j):
            return dot(kv_ref[rows_of(j), :width], q_t)

        def first(j, top):
            tile = score(j)
            scores[j] = tile
            return jnp.maximum(top, fold(jnp.max, tile))

        tile = jnp.where(visible, score(own), NEG_FILL)
        scores[own] = tile
        top = lax.fori_loop(0, own, first, fold(jnp.max, tile))
        top = jnp.max(top, axis=0, keepdims=True) * rate

        def second(j, carry):
            sums, out_t = carry
            prob = jnp.exp2(scores[j] * rate - top)
            low = prob.astype(BF16)
            probs[j] = low
            value_t = kv_ref[rows_of(j), width:].T
            return (sums + fold(jnp.sum, prob), out_t + dot(value_t, low))

        sums, out_t = lax.fori_loop(
            0,
            own + 1,
            second,
            (jnp.zeros((8, lanes_q), F32), jnp.zeros((width, lanes_q), F32)),
        )
        inverse = 1.0 / jnp.sum(sums, axis=0, keepdims=True)
        do_t = do_ref[i].astype(F32).T
        out_low = (out_t * inverse).astype(BF16).astype(F32)
        delta = jnp.sum(do_t * out_low, axis=0, keepdims=True) * inverse
        do_scaled = do_t * inverse
        do_t_low = do_scaled.astype(BF16)
        do_low = do_scaled.T.astype(BF16)

        def third(j, dq_t):
            at = rows_of(j)
            key = kv_ref[at, :width]
            prob = probs[j]
            prob_grad = dot(kv_ref[at, width:], do_t_low)
            ds = (prob.astype(F32) * (prob_grad - delta)).astype(BF16)
            acc[at, :width] += dot(ds, q)
            acc[at, width:] += dot(prob, do_low)
            return dq_t + dot(key.T, ds)

        dq_t = lax.fori_loop(0, own + 1, third, jnp.zeros((width, lanes_q), F32))
        dq_ref[i] = (dq_t * scale).T.astype(BF16)

    quarters, devices, rows = dkv_ref.shape[:3]
    for d in range(devices):
        for u in range(quarters):
            span = pl.ds((d * quarters + u) * rows, rows)
            dkv_ref[u, d, :, :width] = (acc[span, :width] * scale).astype(BF16)
            dkv_ref[u, d, :, width:] = acc[span, width:].astype(BF16)


def spread(weights, width):
    return jnp.repeat(weights, width, axis=-1)[:, None, :]


def states_between(s_own, p_own, tot, width):
    count = lax.axis_size("seq")
    place = lax.axis_index("seq")
    pair = place // 2
    odd = place % 2
    tots = lax.all_gather(tot[:, 0, :], "seq")
    before = jnp.concatenate([jnp.zeros_like(tots[:1]), jnp.cumsum(tots, axis=0)])

    def upto(i):
        return lax.dynamic_index_in_dim(before, jnp.clip(i, 0, count), 0, False)

    swap = [(i, i ^ 1) for i in range(count)]
    other = lax.ppermute(jnp.stack([s_own, p_own]), "seq", swap).astype(F32)
    s_wide, p_wide = s_own.astype(F32), p_own.astype(F32)
    first_s = jnp.where(odd == 1, other[0], s_wide)
    second_s = jnp.where(odd == 1, s_wide, other[0])
    first_p = jnp.where(odd == 1, other[1], p_wide)
    second_p = jnp.where(odd == 1, p_wide, other[1])
    decay_first = spread(jnp.exp(upto(2 * pair + 1) - upto(2 * pair)), width)
    decay_second = spread(jnp.exp(upto(2 * pair + 2) - upto(2 * pair + 1)), width)
    ahead = (first_s * decay_second + second_s).astype(BF16)
    back = (first_p + second_p * decay_first).astype(BF16)
    s_sum = jnp.zeros_like(s_wide)
    p_sum = jnp.zeros_like(p_wide)
    for r in range(1, count // 2):
        ahead = lax.ppermute(ahead, "seq", [(i, i + 2) for i in range(count - 2)])
        back = lax.ppermute(back, "seq", [(i + 2, i) for i in range(count - 2)])
        w_ahead = jnp.exp(jnp.minimum(upto(2 * pair) - upto(2 * (pair - r) + 2), 0.0))
        w_back = jnp.exp(jnp.minimum(upto(2 * (pair + r)) - upto(2 * pair + 2), 0.0))
        s_sum = s_sum + ahead.astype(F32) * spread(w_ahead, width)
        p_sum = p_sum + back.astype(F32) * spread(w_back, width)
    state_in = jnp.where(odd == 1, s_sum * decay_first + first_s, s_sum)
    grad_in = jnp.where(odd == 1, p_sum, p_sum * decay_second + second_p)
    return state_in, grad_in


def per_device(
    ssd_input,
    log_decay,
    input_map,
    output_map,
    ssd_cotangent,
    queries,
    key_rows,
    value_rows,
    attn_cotangent,
    pair_order,
):
    count = lax.axis_size("seq")
    place = lax.axis_index("seq")
    rows, heads, width = ssd_input.shape
    groups, size = input_map.shape[1:]
    per = heads // groups
    span = per * width
    q_rows, q_heads, q_width = queries.shape
    half = q_rows // 2

    kv = lax.all_gather(
        jnp.concatenate([key_rows, value_rows], axis=1), "seq", axis=0, tiled=True
    )

    x = ssd_input.reshape(rows, heads * width)
    dy = ssd_cotangent.reshape(rows, heads * width)
    a = log_decay.reshape(rows, groups, per).transpose(1, 0, 2)
    a_t = a.transpose(0, 2, 1)
    b = input_map.reshape(rows, groups * size)
    c = output_map.reshape(rows, groups * size)

    wide_spec = pl.BlockSpec((rows, span), lambda g: (0, g))
    a_spec = pl.BlockSpec((1, rows, per), lambda g: (g, 0, 0))
    at_spec = pl.BlockSpec((1, per, rows), lambda g: (g, 0, 0))
    map_spec = pl.BlockSpec((rows, size), lambda g: (0, g))
    state_spec = pl.BlockSpec((1, size, span), lambda g: (g, 0, 0))
    state_flops = 4 * rows * heads * width * size
    s_own, p_own, tot = pl.pallas_call(
        state_kernel,
        grid=(groups,),
        in_specs=[wide_spec, wide_spec, a_spec, map_spec, map_spec],
        out_specs=[state_spec, state_spec, pl.BlockSpec((1, 1, per), lambda g: (g, 0, 0))],
        out_shape=[
            jax.ShapeDtypeStruct((groups, size, span), BF16),
            jax.ShapeDtypeStruct((groups, size, span), BF16),
            jax.ShapeDtypeStruct((groups, 1, per), F32),
        ],
        scratch_shapes=[pltpu.VMEM((rows, span), BF16), pltpu.VMEM((rows, span), BF16)],
        compiler_params=pltpu.CompilerParams(vmem_limit_bytes=VMEM_BYTES),
        cost_estimate=pl.CostEstimate(
            flops=state_flops, bytes_accessed=4 * rows * heads * width, transcendentals=0
        ),
    )(x, dy, a, b, c)

    state_in, grad_in = states_between(s_own, p_own, tot, width)

    blocks = 2 * count
    own_first = pair_order[place]
    own = jnp.stack([own_first, blocks - 1 - own_first]).astype(jnp.int32)
    ids = jnp.stack([pair_order, blocks - 1 - pair_order], axis=1).reshape(-1)
    block_ids = jnp.arange(blocks, dtype=jnp.int32)
    where_at = jnp.sum(
        jnp.where(ids[None, :] == block_ids[:, None], block_ids[None, :], 0), axis=1
    ).astype(jnp.int32)

    def by_half(array):
        parts = array.reshape(2, half, q_heads, q_width).transpose(0, 2, 1, 3)
        return parts.reshape(2, q_heads * half, q_width)

    vmem = pl.BlockSpec(memory_space=pltpu.VMEM)
    smem = pl.BlockSpec(memory_space=pltpu.SMEM)
    quarters = lax.axis_size("head")
    lanes_q = q_heads * half
    dq, dkv = pl.pallas_call(
        attention_kernel,
        in_specs=[smem, smem, vmem, vmem, vmem],
        out_specs=[vmem, vmem],
        out_shape=[
            jax.ShapeDtypeStruct((2, lanes_q, q_width), BF16),
            jax.ShapeDtypeStruct((quarters, count, q_rows // quarters, 2 * q_width), BF16),
        ],
        scratch_shapes=[
            pltpu.VMEM((blocks, half, lanes_q), F32),
            pltpu.VMEM((blocks, half, lanes_q), BF16),
            pltpu.VMEM((count * q_rows, 2 * q_width), F32),
        ],
        compiler_params=pltpu.CompilerParams(vmem_limit_bytes=VMEM_BYTES),
        cost_estimate=pl.CostEstimate(
            flops=12 * (blocks + 1) * half * lanes_q * q_width,
            bytes_accessed=4 * count * q_rows * q_width * 4,
            transcendentals=(blocks + 1) * half * lanes_q,
        ),
    )(where_at, own, by_half(queries), by_half(attn_cotangent), kv)

    dkv = lax.psum_scatter(dkv, "head", scatter_dimension=0, tiled=True)[0]
    dkv = lax.psum_scatter(dkv, "seq", scatter_dimension=0, tiled=True)[0]
    dkv = lax.all_gather(dkv, "head", axis=0, tiled=True)
    grad_keys = dkv[:, :q_width]
    grad_values = dkv[:, q_width:]
    grad_queries = (
        dq.reshape(2, q_heads, half, q_width).transpose(0, 2, 1, 3).reshape(queries.shape)
    )

    dx, da, db, dc = pl.pallas_call(
        scan_kernel,
        grid=(groups,),
        in_specs=[
            wide_spec,
            wide_spec,
            a_spec,
            at_spec,
            map_spec,
            map_spec,
            state_spec,
            state_spec,
        ],
        out_specs=[wide_spec, a_spec, map_spec, map_spec],
        out_shape=[
            jax.ShapeDtypeStruct((rows, heads * width), BF16),
            jax.ShapeDtypeStruct((groups, rows, per), F32),
            jax.ShapeDtypeStruct((rows, groups * size), F32),
            jax.ShapeDtypeStruct((rows, groups * size), F32),
        ],
        scratch_shapes=[
            pltpu.VMEM((rows // BLOCK, size, span), BF16),
            pltpu.VMEM((rows, span), BF16),
            pltpu.VMEM((BLOCK, span), BF16),
            pltpu.VMEM((size, span), F32),
            pltpu.VMEM((size, span), F32),
            pltpu.VMEM((BLOCK, BLOCK), F32),
        ],
        compiler_params=pltpu.CompilerParams(vmem_limit_bytes=VMEM_BYTES),
        cost_estimate=pl.CostEstimate(
            flops=5 * state_flops,
            bytes_accessed=8 * rows * heads * width,
            transcendentals=rows * heads * BLOCK,
        ),
    )(x, dy, a, a_t, b, c, state_in, grad_in)

    return (
        dx.reshape(rows, heads, width),
        da.transpose(1, 0, 2).reshape(rows, heads),
        db.reshape(rows, groups, size),
        dc.reshape(rows, groups, size),
        grad_queries,
        grad_keys,
        grad_values,
    )


def solution(mesh):
    return jax.shard_map(
        per_device,
        mesh=mesh,
        in_specs=(
            P("seq", "head", None),
            P("seq", "head"),
            P("seq", "head", None),
            P("seq", "head", None),
            P("seq", "head", None),
            P("seq", "head", None),
            P("seq", None),
            P("seq", None),
            P("seq", "head", None),
            P(),
        ),
        out_specs=(
            P("seq", "head", None),
            P("seq", "head"),
            P("seq", "head", None),
            P("seq", "head", None),
            P("seq", "head", None),
            P("seq", None),
            P("seq", None),
        ),
        check_vma=False,
    )
```

time: 895 us -> 322 us (0.36); the launches traced: 880 us -> 322 us
  local copies, waits for them, and re-layouts: 228 us -> 28.6 us
  matrix products: 162 us -> 0 us
  waiting for transfers between devices: 255 us -> 94.5 us
  loops' own time: 86 us -> 0 us
  other arithmetic: 87.1 us -> 17.3 us
  Pallas kernels: 0 us -> 65.9 us
  blocking collectives: 45 us -> 79.3 us
  starting transfers between devices: 0.86 us -> 21.4 us
    all_gather x4 -> x1, waiting for transfers between devices: 200 us -> 0.01 us  [per_device(): lax.all_gather(jnp.concatenate([key_rows, value_rows], axis=1), 'seq', ax...]
    dot_general x163 -> x0, matrix products: 162 us -> none  [the longest x8 21.9 us: block_advance(): jnp.einsum('tsge,sgep->tgep', weight_grid, x_block, preferred_element_typ...]
    dynamic_slice x113 -> x1, local copies, waits for them, and re-layouts: 127 us -> 0.59 us  [per_device(): own_first = pair_order[place]]
    ppermute x0 -> x7, waiting for transfers between devices: none -> 94.4 us  [the longest x3 52.3 us: states_between(): ahead = lax.ppermute(ahead, 'seq', [(i, i + 2) for i in range(count - 2)])]
    another operation x55 -> x0, loops' own time: 86 us -> none  [the longest x1 26.8 us: per_device(): grad_state = lax.fori_loop(0, seq_count, grad_turn, grad_start)]
    pallas_call x0 -> x3, Pallas kernels: none -> 65.9 us  [the longest x1 35 us: per_device(): pl.pallas_call(scan_kernel, grid=(groups,), in_specs=[wide_spec, wide_spe...]
    reduce_scatter x2, waiting for transfers between devices: 54 us -> 0.01 us  [the longest x1 0.01 us: per_device(): dkv = lax.psum_scatter(dkv, 'head', scatter_dimension=0, tiled=True)[0]]
    dynamic_update_slice x56 -> x0, local copies, waits for them, and re-layouts: 47.1 us -> none  [run_blocks(): lax.scan(block_advance, state_start, (blocked(x_seq), blocked(a_seq), blo...]
  transfers between devices with their start and end apart: 7 -> 10, of which waited for: 4 -> 5; matrix products, arithmetic and copies ran while one was open for 43% -> 8% of each run, Pallas kernels for 0% -> 17%
where the time goes in v1:
time: 322 us
  waiting for transfers between devices  94.5 us (29%)
  blocking collectives  79.3 us (25%)
  Pallas kernels  65.9 us (20%)
  local copies, waits for them, and re-layouts  28.6 us (9%)
  starting transfers between devices  21.4 us (7%)
  other arithmetic  17.3 us (5%)
  between operations  14.8 us (5%)
    all_gather x1, blocking collectives, states_between(): tots = lax.all_gather(tot[:, 0, :], 'seq')  73.3 us
    ppermute x3, waiting for transfers between devices, states_between(): ahead = lax.ppermute(ahead, 'seq', [(i, i + 2) for i in range(count - 2)])  52.3 us
    ppermute x3, waiting for transfers between devices, states_between(): back = lax.ppermute(back, 'seq', [(i + 2, i) for i in range(count - 2)])  42.2 us
    pallas_call x1, Pallas kernels, per_device(): pl.pallas_call(scan_kernel, grid=(groups,), in_specs=[wide_spec, wide_spe...  35 us
    pallas_call x1, Pallas kernels, per_device(): pl.pallas_call(attention_kernel, in_specs=[smem, smem, vmem, vmem, vmem],...  21 us
    ppermute x3, starting transfers between devices, states_between(): ahead = lax.ppermute(ahead, 'seq', [(i, i + 2) for i in range(count - 2)])  14.5 us
    reshape x1, local copies, waits for them, and re-layouts, per_device(): dy = ssd_cotangent.reshape(rows, heads * width)  13.4 us
    pallas_call x1, Pallas kernels, per_device(): pl.pallas_call(state_kernel, grid=(groups,), in_specs=[wide_spec, wide_sp...  9.87 us
  transfers between devices with their start and end apart: 10, of which 5 were waited for; matrix products, arithmetic and copies ran while one was open for 8% of the time, Pallas kernels for 17%

profile of v1, /device:TPU:0, one launch (start us, length us, event | category | flops | bytes accessed | tf_op | source)
XLA Modules:
  0.0 321.8 jit_solution(14734797146339395304)
XLA Ops:
  8.3 13.4 %copy_bitcast_fusion = (bf16[512,4096]{1,0:T(8,128)(2,1)}, bf16[512,4096]{1,0:T(8,128)(2,1)}) fusion(bf16[64,8,32,128]{3,2,1,0:T(8,128)(2,1)} %bitcast.128, bf16[64,8,32,128]{3,2,1,0:T(8,128)(2,1)} %bitcast.129), kind=kLoop, calls=%fused_computation | loop fusion | bytes 16777216 | tf_op jit(solution)/shard_map/reshape | solution.py:335
  21.8 9.9 %shard_map.153 = (bf16[2,128,2048]{2,1,0:T(8,128)(2,1)}, bf16[2,128,2048]{2,1,0:T(8,128)(2,1)}, f32[2,1,16]{2,1,0:T(1,128)S(1)}) custom-call(bf16[512,4096]{1,0:T(8,128)(2,1)} %get-tuple-element.38.x_ref, bf16[512,4096]{1,0:T(8,128)(2,1)} %get-tuple-element.37.dy_ref, f32[2,512,16]{2,1,0:T(8,128)S(1)} %copy.38.a_ref, ...), custom_call_target="tpu_custom_call" | custom-call | flops 1073741824 | bytes 8388608 | tf_op jit(solution)/shard_map/pallas_call | solution.py:347
  31.7 3.1 pad_maximum_fusion
  34.9 3.0 collective-permute-start
  38.7 73.3 %all-gather = f32[16,1,16]{2,1,0:T(1,128)S(1)} all-gather(f32[2,1,16]{2,1,0:T(1,128)S(1)} %get-tuple-element.18), channel_id=2, replica_groups=mesh['seq'=8,'head'=4] {'seq'}, dimensions={0}, use_global_device_ids=true | all-gather | bytes 1152 | tf_op jit(solution)/shard_map/all_gather | solution.py:278
  112.1 2.2 convert_element_type.33
  114.8 1.5 copy-done.4
  116.4 1.3 collective-permute-start.4
  117.7 22.0 %collective-permute-done.4 = bf16[2,128,2048]{2,1,0:T(8,128)(2,1)S(1)} collective-permute-done((bf16[2,128,2048]{2,1,0:T(8,128)(2,1)S(1)}, bf16[2,128,2048]{2,1,0:T(8,128)(2,1)S(1)}, u32[]{:S(2)}, u32[]{:S(2)}) %collective-permute-start.4) | collective-permute-done | bytes 1048608 | tf_op jit(solution)/shard_map/ppermute | solution.py:299
  139.7 1.3 collective-permute-start.5
  142.6 20.2 %collective-permute-done.5 = bf16[2,128,2048]{2,1,0:T(8,128)(2,1)} collective-permute-done((bf16[2,128,2048]{2,1,0:T(8,128)(2,1)S(1)}, bf16[2,128,2048]{2,1,0:T(8,128)(2,1)}, u32[]{:S(2)}, u32[]{:S(2)}) %collective-permute-start.5) | collective-permute-done | bytes 1048608 | tf_op jit(solution)/shard_map/ppermute | solution.py:299
  162.8 1.3 collective-permute-start.6
  165.0 21.0 %shard_map.155 = (bf16[2,512,128]{2,1,0:T(8,128)(2,1)S(1)}, bf16[4,8,128,256]{3,2,1,0:T(8,128)(2,1)}) custom-call(s32[16]{0:T(128)S(1)} %select_reduce_fusion.place_ref, s32[2]{0:T(128)S(1)} %pad_add_fusion.1.own_ref, bf16[2,512,128]{2,1,0:T(8,128)(2,1)S(1)} %bitcast.120, bf16[2,512,128]{2,1,0:T(8,128)(2,1)S(1)} %bitcast.121, ...), custom_call_target="tpu_custom_call" | custom-call | flops 3422552064 | bytes 8388608 | tf_op jit(solution)/shard_map/pallas_call | solution.py:383
  187.2 5.7 %add_select_fusion = (f32[2,128,2048]{2,1,0:T(8,128)}, bf16[2,128,2048]{2,1,0:T(8,128)(2,1)S(1)}) fusion(bf16[2,128,2048]{2,1,0:T(8,128)(2,1)} %collective-permute-done.6, bf16[2,128,2048]{2,1,0:T(8,128)(2,1)} %collective-permute-done.5, bf16[2,128,2048]{2,1,0:T(8,128)(2,1)S(1)} %collective-permute-done.4, f32[2,2,128,2048]{3,2,1,0:T(8,128)} %copy-done.4, ...), kind=kLoop, calls=%fused_computation.13 | loop fusion | flops 9961472 | bytes 12648449 | tf_op jit(solution)/shard_map/jit(_where)/select_n | solution.py:305
  192.9 4.6 %collective-permute-start.1 = (bf16[2,128,2048]{2,1,0:T(8,128)(2,1)S(1)}, bf16[2,128,2048]{2,1,0:T(8,128)(2,1)S(1)}, u32[]{:S(2)}, u32[]{:S(2)}) collective-permute-start(bf16[2,128,2048]{2,1,0:T(8,128)(2,1)S(1)} %get-tuple-element.26), channel_id=1, source_target_pairs={{0,8},{4,12},{8,16},{12,20},{16,24},{20,28},{1,9},{5,13},{9,17},{1... | collective-permute-start | bytes 3145736 | tf_op jit(solution)/shard_map/ppermute | solution.py:298
  197.5 18.8 %collective-permute-done.1 = bf16[2,128,2048]{2,1,0:T(8,128)(2,1)S(1)} collective-permute-done((bf16[2,128,2048]{2,1,0:T(8,128)(2,1)S(1)}, bf16[2,128,2048]{2,1,0:T(8,128)(2,1)S(1)}, u32[]{:S(2)}, u32[]{:S(2)}) %collective-permute-start.1) | collective-permute-done | bytes 1048608 | tf_op jit(solution)/shard_map/ppermute | solution.py:298
  216.3 4.4 %collective-permute-start.2 = (bf16[2,128,2048]{2,1,0:T(8,128)(2,1)S(1)}, bf16[2,128,2048]{2,1,0:T(8,128)(2,1)S(1)}, u32[]{:S(2)}, u32[]{:S(2)}) collective-permute-start(bf16[2,128,2048]{2,1,0:T(8,128)(2,1)S(1)} %collective-permute-done.1), channel_id=1, source_target_pairs={{0,8},{4,12},{8,16},{12,20},{16,24},{20,28},{1,9},{5,13},{9,17},{1... | collective-permute-start | bytes 3145736 | tf_op jit(solution)/shard_map/ppermute | solution.py:298
  220.8 18.9 %collective-permute-done.2 = bf16[2,128,2048]{2,1,0:T(8,128)(2,1)S(1)} collective-permute-done((bf16[2,128,2048]{2,1,0:T(8,128)(2,1)S(1)}, bf16[2,128,2048]{2,1,0:T(8,128)(2,1)S(1)}, u32[]{:S(2)}, u32[]{:S(2)}) %collective-permute-start.2) | collective-permute-done | bytes 1048608 | tf_op jit(solution)/shard_map/ppermute | solution.py:298
  239.6 5.4 %collective-permute-start.3 = (bf16[2,128,2048]{2,1,0:T(8,128)(2,1)S(1)}, bf16[2,128,2048]{2,1,0:T(8,128)(2,1)}, u32[]{:S(2)}, u32[]{:S(2)}) collective-permute-start(bf16[2,128,2048]{2,1,0:T(8,128)(2,1)S(1)} %collective-permute-done.2), channel_id=1, source_target_pairs={{0,8},{4,12},{8,16},{12,20},{16,24},{20,28},{1,9},{5,13},{9,17},{1... | collective-permute-start | bytes 3145736 | tf_op jit(solution)/shard_map/ppermute | solution.py:298
  246.3 14.6 %collective-permute-done.3 = bf16[2,128,2048]{2,1,0:T(8,128)(2,1)} collective-permute-done((bf16[2,128,2048]{2,1,0:T(8,128)(2,1)S(1)}, bf16[2,128,2048]{2,1,0:T(8,128)(2,1)}, u32[]{:S(2)}, u32[]{:S(2)}) %collective-permute-start.3) | collective-permute-done | bytes 1048608 | tf_op jit(solution)/shard_map/ppermute | solution.py:298
  260.9 4.3 %add_select_fusion.1.s_in = f32[2,128,2048]{2,1,0:T(8,128)} fusion(bf16[2,128,2048]{2,1,0:T(8,128)(2,1)} %collective-permute-done.3, bf16[2,128,2048]{2,1,0:T(8,128)(2,1)S(1)} %collective-permute-done.2, bf16[2,128,2048]{2,1,0:T(8,128)(2,1)S(1)} %collective-permute-done.1, bf16[2,128,2048]{2,1,0:T(8,128)(2,1)S(1)} %copy-done.5, ...), kind=kLoop, calls=%fused_computation.14 | loop fusion | flops 6815744 | bytes 8454145 | tf_op jit(solution)/shard_map/jit(_where)/select_n | solution.py:304
  265.2 35.0 %shard_map.154 = (bf16[512,4096]{1,0:T(8,128)(2,1)}, f32[2,512,16]{2,1,0:T(8,128)S(1)}, f32[512,256]{1,0:T(8,128)S(1)}, f32[512,256]{1,0:T(8,128)S(1)}) custom-call(bf16[512,4096]{1,0:T(8,128)(2,1)} %get-tuple-element.38.x_ref, bf16[512,4096]{1,0:T(8,128)(2,1)} %get-tuple-element.37.dy_ref, f32[2,512,16]{2,1,0:T(8,128)} %copy-done, ...), custom_call_target="tpu_custom_call" | custom-call | flops 5368709120 | bytes 16777216 | tf_op jit(solution)/shard_map/pallas_call | solution.py:413
  300.2 5.5 %copy.56 = bf16[64,8,32,128]{3,2,1,0:T(8,128)(2,1)} copy(bf16[64,8,32,128]{3,1,2,0:T(8,128)(2,1)} %bitcast.127) | data formatting | bytes 8388608
  308.6 6.0 %all-gather.1 = bf16[1,512,256]{2,1,0:T(8,128)(2,1)S(1)} all-gather(bf16[1,128,256]{2,1,0:T(8,128)(2,1)} %reduce-scatter.5.cloned.1.call-done), channel_id=3, replica_groups=mesh['seq'=8,'head'=4] {'head'}, dimensions={1}, use_global_device_ids=true | all-gather | bytes 327680 | tf_op jit(solution)/shard_map/all_gather | solution.py:406
  (75 shorter events, 10.4 us)
Async XLA Ops:
  7.2 157.8 %all-gather.4.cloned.1.call-start = ((), (), s32[]{:S(2)}) async-start(), calls=%async_computation.2 | async-start | bytes 2359296 | tf_op jit(solution)/shard_map/all_gather | solution.py:330
  8.3 13.6 %copy-start = (f32[2,512,16]{2,1,0:T(8,128)}, f32[2,512,16]{2,1,0:T(8,128)S(1)}, u32[]{:S(2)}) copy-start(f32[2,512,16]{2,1,0:T(8,128)S(1)} %copy.38.a_ref) | copy-start | bytes 196612
  8.3 13.4 %copy-start.7 = (f32[512,2,128]{2,1,0:T(2,128)S(1)}, f32[512,2,128]{2,1,0:T(2,128)}, u32[]{:S(2)}) copy-start(f32[512,2,128]{2,1,0:T(2,128)} %param.13) | copy-start | bytes 1572868
  8.3 13.4 %copy-start.8 = (f32[512,2,128]{2,1,0:T(2,128)S(1)}, f32[512,2,128]{2,1,0:T(2,128)}, u32[]{:S(2)}) copy-start(f32[512,2,128]{2,1,0:T(2,128)} %param.12) | copy-start | bytes 1572868
  21.8 9.9 %copy-start.1 = (f32[512,256]{1,0:T(8,128)}, f32[512,256]{1,0:T(8,128)S(1)}, u32[]{:S(2)}) copy-start(f32[512,256]{1,0:T(8,128)S(1)} %get-tuple-element.39.c_ref) | copy-start | bytes 1572868
  21.8 9.9 %copy-start.2 = (f32[512,256]{1,0:T(8,128)}, f32[512,256]{1,0:T(8,128)S(1)}, u32[]{:S(2)}) copy-start(f32[512,256]{1,0:T(8,128)S(1)} %get-tuple-element.40.b_ref) | copy-start | bytes 1572868
  31.7 6.1 %copy-start.11 = (bf16[512,128]{1,0:T(8,128)(2,1)S(1)}, bf16[512,128]{1,0:T(8,128)(2,1)}, u32[]{:S(2)}) copy-start(bf16[512,128]{1,0:T(8,128)(2,1)} %param.17) | copy-start | bytes 393220
  31.7 6.1 %copy-start.12 = (bf16[512,128]{1,0:T(8,128)(2,1)S(1)}, bf16[512,128]{1,0:T(8,128)(2,1)}, u32[]{:S(2)}) copy-start(bf16[512,128]{1,0:T(8,128)(2,1)} %param.16) | copy-start | bytes 393220
  34.9 77.3 %collective-permute-start = (bf16[2,2,128,2048]{3,2,1,0:T(8,128)(2,1)}, bf16[2,2,128,2048]{3,2,1,0:T(8,128)(2,1)}, u32[]{:S(2)}, u32[]{:S(2)}) collective-permute-start(bf16[2,2,128,2048]{3,2,1,0:T(8,128)(2,1)} %pad_maximum_fusion), channel_id=1, source_target_pairs={{0,4},{4,0},{8,12},{12,8},{16,20},{20,16},{24,28},{28,24},{1,5},{5... | collective-permute-start | bytes 6291464 | tf_op jit(solution)/shard_map/ppermute | solution.py:285
  38.6 207.7 %reduce-scatter.3.cloned.1.call-start = ((), (), s32[]{:S(2)}) async-start(), calls=%async_computation.3 | async-start | bytes 2621440 | tf_op jit(solution)/shard_map/reduce_scatter | solution.py:404
  112.1 2.2 copy-start.6
  114.3 2.0 copy-start.4
  114.4 26.6 %copy-start.13 = (s32[8]{0:T(128)S(1)}, s32[8]{0:T(128)}, u32[]{:S(2)}) copy-start(s32[8]{0:T(128)} %param.19) | copy-start | bytes 100
  114.4 50.4 %copy-start.9 = (bf16[512,2,128]{2,1,0:T(2,128)(2,1)S(1)}, bf16[512,2,128]{2,1,0:T(2,128)(2,1)}, u32[]{:S(2)}) copy-start(bf16[512,2,128]{2,1,0:T(2,128)(2,1)} %param.15) | copy-start | bytes 786436
  114.4 50.5 %copy-start.10 = (bf16[512,2,128]{2,1,0:T(2,128)(2,1)S(1)}, bf16[512,2,128]{2,1,0:T(2,128)(2,1)}, u32[]{:S(2)}) copy-start(bf16[512,2,128]{2,1,0:T(2,128)(2,1)} %param.18) | copy-start | bytes 786436
  116.4 23.3 %collective-permute-start.4 = (bf16[2,128,2048]{2,1,0:T(8,128)(2,1)S(1)}, bf16[2,128,2048]{2,1,0:T(8,128)(2,1)S(1)}, u32[]{:S(2)}, u32[]{:S(2)}) collective-permute-start(bf16[2,128,2048]{2,1,0:T(8,128)(2,1)S(1)} %fusion.3), channel_id=1, source_target_pairs={{8,0},{12,4},{16,8},{20,12},{24,16},{28,20},{9,1},{13,5},{17,9},{2... | collective-permute-start | bytes 3145736 | tf_op jit(solution)/shard_map/ppermute | solution.py:299
  139.7 23.1 %collective-permute-start.5 = (bf16[2,128,2048]{2,1,0:T(8,128)(2,1)S(1)}, bf16[2,128,2048]{2,1,0:T(8,128)(2,1)}, u32[]{:S(2)}, u32[]{:S(2)}) collective-permute-start(bf16[2,128,2048]{2,1,0:T(8,128)(2,1)S(1)} %collective-permute-done.4), channel_id=1, source_target_pairs={{8,0},{12,4},{16,8},{20,12},{24,16},{28,20},{9,1},{13,5},{17,9},{2... | collective-permute-start | bytes 3145736 | tf_op jit(solution)/shard_map/ppermute | solution.py:299
  162.8 23.5 %collective-permute-start.6 = (bf16[2,128,2048]{2,1,0:T(8,128)(2,1)}, bf16[2,128,2048]{2,1,0:T(8,128)(2,1)}, u32[]{:S(2)}, u32[]{:S(2)}) collective-permute-start(bf16[2,128,2048]{2,1,0:T(8,128)(2,1)} %collective-permute-done.5), channel_id=1, source_target_pairs={{8,0},{12,4},{16,8},{20,12},{24,16},{28,20},{9,1},{13,5},{17,9},{2... | collective-permute-start | bytes 3145736 | tf_op jit(solution)/shard_map/ppermute | solution.py:299
  186.0 1.2 copy-start.5
  186.0 122.5 %reduce-scatter.5.cloned.1.call-start = ((), (), s32[]{:S(2)}) async-start(), calls=%async_computation.4 | async-start | bytes 589824 | tf_op jit(solution)/shard_map/reduce_scatter | solution.py:405
  192.9 23.4 %collective-permute-start.1 = (bf16[2,128,2048]{2,1,0:T(8,128)(2,1)S(1)}, bf16[2,128,2048]{2,1,0:T(8,128)(2,1)S(1)}, u32[]{:S(2)}, u32[]{:S(2)}) collective-permute-start(bf16[2,128,2048]{2,1,0:T(8,128)(2,1)S(1)} %get-tuple-element.26), channel_id=1, source_target_pairs={{0,8},{4,12},{8,16},{12,20},{16,24},{20,28},{1,9},{5,13},{9,17},{1... | collective-permute-start | bytes 3145736 | tf_op jit(solution)/shard_map/ppermute | solution.py:298
  216.3 23.3 %collective-permute-start.2 = (bf16[2,128,2048]{2,1,0:T(8,128)(2,1)S(1)}, bf16[2,128,2048]{2,1,0:T(8,128)(2,1)S(1)}, u32[]{:S(2)}, u32[]{:S(2)}) collective-permute-start(bf16[2,128,2048]{2,1,0:T(8,128)(2,1)S(1)} %collective-permute-done.1), channel_id=1, source_target_pairs={{0,8},{4,12},{8,16},{12,20},{16,24},{20,28},{1,9},{5,13},{9,17},{1... | collective-permute-start | bytes 3145736 | tf_op jit(solution)/shard_map/ppermute | solution.py:298
  239.6 21.3 %collective-permute-start.3 = (bf16[2,128,2048]{2,1,0:T(8,128)(2,1)S(1)}, bf16[2,128,2048]{2,1,0:T(8,128)(2,1)}, u32[]{:S(2)}, u32[]{:S(2)}) collective-permute-start(bf16[2,128,2048]{2,1,0:T(8,128)(2,1)S(1)} %collective-permute-done.2), channel_id=1, source_target_pairs={{0,8},{4,12},{8,16},{12,20},{16,24},{20,28},{1,9},{5,13},{9,17},{1... | collective-permute-start | bytes 3145736 | tf_op jit(solution)/shard_map/ppermute | solution.py:298
  260.9 4.3 %copy-start.3 = (f32[512,32]{0,1:T(8,128)S(1)}, f32[512,32]{0,1:T(8,128)}, u32[]{:S(2)}) copy-start(f32[512,32]{0,1:T(8,128)} %param.11) | copy-start | bytes 196612
Sparse Core Ops, SparseCore 0:
  38.7 63.5 all-gather.3
  186.1 30.7 reduce-scatter.2
  246.4 59.3 reduce-scatter.4

commit v2 on v1

v2 whole, which is shorter than its diff:
```python
import functools
import math

import jax
import jax.numpy as jnp
from jax import lax
from jax.experimental import pallas as pl
from jax.experimental.pallas import tpu as pltpu
from jax.sharding import PartitionSpec as P

BLOCK = 128
HIGHEST = lax.Precision.HIGHEST
NEG_FILL = -1e30
F32 = jnp.float32
BF16 = jnp.bfloat16
VMEM_BYTES = 52 * 1024 * 1024


def dot(a, b):
    return jnp.dot(a, b, preferred_element_type=F32)


def dot_t(a, b):
    return lax.dot_general(a, b, (((1,), (1,)), ((), ())), preferred_element_type=F32)


def dot_hi(a, b):
    return jnp.dot(a, b, preferred_element_type=F32, precision=HIGHEST)


def iota2(shape, dim):
    return lax.broadcasted_iota(jnp.int32, shape, dim)


def lower_ones():
    shape = (BLOCK, BLOCK)
    return (iota2(shape, 0) >= iota2(shape, 1)).astype(F32)


def upper_ones():
    shape = (BLOCK, BLOCK)
    return (iota2(shape, 0) <= iota2(shape, 1)).astype(F32)


def state_kernel(x_ref, dy_ref, a_ref, b_ref, c_ref, sp_ref, tx, ey):
    rows, heads = a_ref.shape[1:]
    width = x_ref.shape[1] // heads
    lower = lower_ones()
    offset = jnp.zeros((1, heads), F32)
    cums = []
    for k in range(rows // BLOCK):
        cum = dot_hi(lower, a_ref[0, pl.ds(k * BLOCK, BLOCK), :])
        cums.append(cum + offset)
        offset = offset + cum[BLOCK - 1 :, :]
    for k, cum in enumerate(cums):
        span = pl.ds(k * BLOCK, BLOCK)
        tail = jnp.exp(offset - cum)
        head_decay = jnp.exp(cum)
        for h in range(heads):
            lanes = pl.ds(h * width, width)
            tx[span, lanes] = (x_ref[span, lanes].astype(F32) * tail[:, h : h + 1]).astype(BF16)
            ey[span, lanes] = (
                dy_ref[span, lanes].astype(F32) * head_decay[:, h : h + 1]
            ).astype(BF16)
    b_t = b_ref[0].T.astype(BF16)
    c_t = c_ref[0].T.astype(BF16)
    chunks, _, _, step = sp_ref.shape
    for at in range(chunks):
        lanes = pl.ds(at * step, step)
        sp_ref[at, 0] = dot(b_t, tx[:, lanes]).astype(BF16)
        sp_ref[at, 1] = dot(c_t, ey[:, lanes]).astype(BF16)


def scan_kernel(
    pairs,
    x_ref,
    dy_ref,
    a_ref,
    at_ref,
    b_ref,
    c_ref,
    sp_ref,
    w_ref,
    dx_ref,
    da_ref,
    db_ref,
    dc_ref,
    y_in,
    f_in,
    b_in,
    f_out,
    b_out,
    states,
    tails,
    s_all,
    ds_all,
    gts,
    dgt,
    maps_low,
    maps_t,
    y_send,
    y_recv,
    f_send,
    f_recv,
    b_send,
    b_recv,
):
    chunks, rows, heads = a_ref.shape
    groups, _, size = b_ref.shape
    per_group = chunks // groups
    width = x_ref.shape[1] // (chunks * heads)
    count = rows // BLOCK
    me = lax.axis_index("seq")
    pair = me // 2
    odd = me - 2 * pair
    partner = me + 1 - 2 * odd
    up = me + 2
    down = me - 2
    has_up = pair < pairs - 1
    has_down = pair > 0

    barrier = pltpu.get_barrier_semaphore()

    def greet(device):
        pl.semaphore_signal(
            barrier, inc=1, device_id={"seq": device}, device_id_type=pl.DeviceIdType.MESH
        )

    greet(partner)
    pl.when(has_up)(lambda: greet(up))
    pl.when(has_down)(lambda: greet(down))
    pl.semaphore_wait(barrier, 1 + has_up.astype(jnp.int32) + has_down.astype(jnp.int32))

    def remote(src, dst, send, recv, c, device):
        return pltpu.make_async_remote_copy(
            src_ref=src.at[c],
            dst_ref=dst.at[c],
            send_sem=send.at[c],
            recv_sem=recv.at[c],
            device_id={"seq": device},
            device_id_type=pl.DeviceIdType.MESH,
        )

    def swap(c):
        return remote(sp_ref, y_in, y_send, y_recv, c, partner)

    def climb(c):
        return remote(f_out, f_in, f_send, f_recv, c, up)

    def descend(c):
        return remote(b_out, b_in, b_send, b_recv, c, down)

    ahead = min(2, chunks)
    for c in range(ahead):
        swap(c).start()

    lower = lower_ones()
    upper = upper_ones()
    causal = iota2((BLOCK, BLOCK), 0) <= iota2((BLOCK, BLOCK), 1)
    db_ref[...] = jnp.zeros_like(db_ref)
    dc_ref[...] = jnp.zeros_like(dc_ref)
    dgt[...] = jnp.zeros_like(dgt)

    def prepare(at, carry):
        g = at // count
        span = pl.ds(pl.multiple_of((at - g * count) * BLOCK, BLOCK), BLOCK)
        b_wide = b_ref[g, span, :]
        c_wide = c_ref[g, span, :]
        gts[at] = lax.dot_general(
            b_wide, c_wide, (((1,), (1,)), ((), ())), preferred_element_type=F32, precision=HIGHEST
        )
        maps_low[at, 0] = b_wide.astype(BF16)
        maps_low[at, 1] = c_wide.astype(BF16)
        maps_t[at, 0] = b_wide.T.astype(BF16)
        maps_t[at, 1] = c_wide.T.astype(BF16)
        return carry

    lax.fori_loop(0, groups * count, prepare, 0)
    is_odd = odd == 1

    def forward_link(c):
        own = sp_ref[c, 0].astype(F32)
        other = y_in[c, 0].astype(F32)
        first = jnp.where(is_odd, other, own)
        second = jnp.where(is_odd, own, other)
        w_first = w_ref[c, 0:1, :]
        w_second = w_ref[c, 1:2, :]
        f_out[c] = (first * w_second + second).astype(BF16)
        s_all[c] = jnp.where(is_odd, first, 0.0)

        @pl.when(has_down)
        def _():
            climb(c).wait_recv()
            arrived = f_in[c].astype(F32)
            s_all[c] = jnp.where(is_odd, arrived * w_first + first, arrived)
            total = first * w_second + second + arrived * (w_first * w_second)
            f_out[c] = total.astype(BF16)

        pl.when(has_up)(lambda: climb(c).start())

    def backward_link(c):
        own = sp_ref[c, 1].astype(F32)
        other = y_in[c, 1].astype(F32)
        first = jnp.where(is_odd, other, own)
        second = jnp.where(is_odd, own, other)
        w_first = w_ref[c, 0:1, :]
        w_second = w_ref[c, 1:2, :]
        b_out[c] = (first + second * w_first).astype(BF16)
        ds_all[c] = jnp.where(is_odd, 0.0, second)

        @pl.when(has_up)
        def _():
            descend(c).wait_recv()
            arrived = b_in[c].astype(F32)
            ds_all[c] = jnp.where(is_odd, arrived, arrived * w_second + second)
            total = first + second * w_first + arrived * (w_first * w_second)
            b_out[c] = total.astype(BF16)

        pl.when(has_down)(lambda: descend(c).start())

    def scan_chunk(c):
        g = c // per_group
        base = c * (heads * width)

        def lanes_of(h):
            return pl.ds(pl.multiple_of(base + h * width, width), width)

        def forward(k, carry):
            span = pl.ds(pl.multiple_of(k * BLOCK, BLOCK), BLOCK)
            cum = dot_hi(lower, a_ref[c, span, :])
            last = cum[BLOCK - 1 :, :]
            tail = jnp.exp(last - cum)
            whole = jnp.exp(last)
            b_t = maps_t[g * count + k, 0]
            for h in range(heads):
                lanes = pl.ds(h * width, width)
                tail_x = (x_ref[span, lanes_of(h)].astype(F32) * tail[:, h : h + 1]).astype(BF16)
                tails[span, lanes] = tail_x
                now = s_all[c, :, lanes]
                states[k, :, lanes] = now.astype(BF16)
                s_all[c, :, lanes] = now * whole[:, h : h + 1] + dot(b_t, tail_x)
            return carry

        lax.fori_loop(0, count, forward, 0)

        def backward(turn, carry):
            k = count - 1 - turn
            at = g * count + k
            span = pl.ds(pl.multiple_of(k * BLOCK, BLOCK), BLOCK)
            cum = dot_hi(lower, a_ref[c, span, :])
            cum_t = dot_hi(at_ref[c, :, span], upper)
            last = cum[BLOCK - 1 :, :]
            tail = jnp.exp(last - cum)
            whole = jnp.exp(last)
            grow = jnp.exp(cum)
            b_low = maps_low[at, 0]
            c_low = maps_low[at, 1]
            c_t = maps_t[at, 1]
            gt = gts[at]
            columns = jnp.zeros((BLOCK, heads), F32)
            row_sums = jnp.zeros((heads, BLOCK), F32)
            totals = jnp.zeros((heads, BLOCK), F32)
            column_at = iota2((BLOCK, heads), 1)
            row_at = iota2((heads, BLOCK), 0)
            db = jnp.zeros((BLOCK, size), F32)
            dc = jnp.zeros((BLOCK, size), F32)
            dg = jnp.zeros((BLOCK, BLOCK), F32)
            for h in range(heads):
                lanes = pl.ds(h * width, width)
                x_h = x_ref[span, lanes_of(h)]
                dy_h = dy_ref[span, lanes_of(h)]
                tail_x = tails[span, lanes]
                state = states[k, :, lanes]
                ds_wide = ds_all[c, :, lanes]
                ds_low = ds_wide.astype(BF16)
                decay = jnp.exp(
                    jnp.where(causal, cum_t[h : h + 1, :] - cum[:, h : h + 1], NEG_FILL)
                )
                t1 = dot_t(x_h, dy_h) * decay
                dg = dg + t1
                mt = t1 * gt
                from_state = dot(b_low, ds_low)
                dx = dot((gt * decay).astype(BF16), dy_h) + from_state * tail[:, h : h + 1]
                dx_ref[span, lanes_of(h)] = dx.astype(BF16)
                edy_h = (dy_h.astype(F32) * grow[:, h : h + 1]).astype(BF16)
                r2 = tail_x.astype(F32) * from_state
                column = jnp.sum(
                    edy_h.astype(F32) * dot(c_low, state) - r2 - mt, axis=1, keepdims=True
                )
                columns = jnp.where(column_at == h, column, columns)
                row_sums = jnp.where(row_at == h, jnp.sum(mt, axis=0, keepdims=True), row_sums)
                total = jnp.sum(r2, axis=0, keepdims=True) + whole[:, h : h + 1] * jnp.sum(
                    ds_wide * state.astype(F32), axis=0, keepdims=True
                )
                totals = jnp.where(row_at == h, total, totals)
                dc = dc + dot_t(edy_h, state)
                db = db + dot_t(tail_x, ds_low)
                ds_all[c, :, lanes] = ds_wide * whole[:, h : h + 1] + dot(c_t, edy_h)
            dgt[at] += dg
            db_ref[g, span, :] += db
            dc_ref[g, span, :] += dc
            total = jnp.sum(totals, axis=1, keepdims=True)
            row_sums = row_sums + jnp.where(iota2((heads, BLOCK), 1) == BLOCK - 1, total, 0.0)
            da_ref[c, span, :] = dot_hi(upper, columns + row_sums.T)
            return carry

        lax.fori_loop(0, count, backward, 0)

    def turn(t, carry):
        @pl.when(t < chunks)
        def _():
            swap(t).wait_recv()

        @pl.when(t + ahead < chunks)
        def _():
            swap(t + ahead).start()

        cf = t - pair

        @pl.when((cf >= 0) & (cf < chunks))
        def _():
            forward_link(cf)

        cb = t - (pairs - 1 - pair)

        @pl.when((cb >= 0) & (cb < chunks))
        def _():
            backward_link(cb)

        done = t - (pairs - 1)

        @pl.when(done >= 0)
        def _():
            scan_chunk(done)

        return carry

    lax.fori_loop(0, chunks + pairs - 1, turn, 0)

    def finish(at, carry):
        g = at // count
        span = pl.ds(pl.multiple_of((at - g * count) * BLOCK, BLOCK), BLOCK)
        dg = dgt[at]
        db_ref[g, span, :] += dot_hi(dg, c_ref[g, span, :])
        dc_ref[g, span, :] += dot_hi(dg.T, b_ref[g, span, :])
        return carry

    lax.fori_loop(0, groups * count, finish, 0)

    def settle(c, carry):
        swap(c).wait_send()
        pl.when(has_up)(lambda: climb(c).wait_send())
        pl.when(has_down)(lambda: descend(c).wait_send())
        return carry

    lax.fori_loop(0, chunks, settle, 0)


def attention_kernel(
    place_ref, own_ref, q_ref, do_ref, kv_ref, dq_ref, dkv_ref, scores, probs, acc
):
    halves, lanes_q, width = q_ref.shape
    half = kv_ref.shape[0] // place_ref.shape[0]
    scale = width ** (-0.5)
    rate = scale * math.log2(math.e)
    acc[...] = jnp.zeros_like(acc)
    visible = iota2((half, lanes_q), 0) <= lax.rem(iota2((half, lanes_q), 1), half)

    def rows_of(j):
        return pl.ds(pl.multiple_of(place_ref[j] * half, half), half)

    def fold(op, tile):
        return op(tile.reshape(half // 8, 8, lanes_q), axis=0)

    for i in range(halves):
        own = own_ref[i]
        q = q_ref[i]
        q_t = q.T

        def score(j):
            return dot(kv_ref[rows_of(j), :width], q_t)

        def first(j, top):
            tile = score(j)
            scores[j] = tile
            return jnp.maximum(top, fold(jnp.max, tile))

        tile = jnp.where(visible, score(own), NEG_FILL)
        scores[own] = tile
        top = lax.fori_loop(0, own, first, fold(jnp.max, tile))
        top = jnp.max(top, axis=0, keepdims=True) * rate

        def second(j, carry):
            sums, out_t = carry
            prob = jnp.exp2(scores[j] * rate - top)
            low = prob.astype(BF16)
            probs[j] = low
            value_t = kv_ref[rows_of(j), width:].T
            return (sums + fold(jnp.sum, prob), out_t + dot(value_t, low))

        sums, out_t = lax.fori_loop(
            0,
            own + 1,
            second,
            (jnp.zeros((8, lanes_q), F32), jnp.zeros((width, lanes_q), F32)),
        )
        inverse = 1.0 / jnp.sum(sums, axis=0, keepdims=True)
        do_t = do_ref[i].astype(F32).T
        out_low = (out_t * inverse).astype(BF16).astype(F32)
        delta = jnp.sum(do_t * out_low, axis=0, keepdims=True) * inverse
        do_scaled = do_t * inverse
        do_t_low = do_scaled.astype(BF16)
        do_low = do_scaled.T.astype(BF16)

        def third(j, dq_t):
            at = rows_of(j)
            key = kv_ref[at, :width]
            prob = probs[j]
            prob_grad = dot(kv_ref[at, width:], do_t_low)
            ds = (prob.astype(F32) * (prob_grad - delta)).astype(BF16)
            acc[at, :width] += dot(ds, q)
            acc[at, width:] += dot(prob, do_low)
            return dq_t + dot(key.T, ds)

        dq_t = lax.fori_loop(0, own + 1, third, jnp.zeros((width, lanes_q), F32))
        dq_ref[i] = (dq_t * scale).T.astype(BF16)

    quarters, devices, rows = dkv_ref.shape[:3]
    for d in range(devices):
        for u in range(quarters):
            span = pl.ds((d * quarters + u) * rows, rows)
            dkv_ref[u, d, :, :width] = (acc[span, :width] * scale).astype(BF16)
            dkv_ref[u, d, :, width:] = acc[span, width:].astype(BF16)


def pair_decays(log_decay, chunks, width):
    pair = lax.axis_index("seq") // 2
    tots = lax.all_gather(jnp.sum(log_decay, axis=0, keepdims=True), "seq")
    own = lax.dynamic_slice_in_dim(tots[:, 0], 2 * pair, 2, 0)
    decays = jnp.repeat(jnp.exp(own), width, axis=1)
    return decays.reshape(2, chunks, -1).transpose(1, 0, 2)


def per_device(
    ssd_input,
    log_decay,
    input_map,
    output_map,
    ssd_cotangent,
    queries,
    key_rows,
    value_rows,
    attn_cotangent,
    pair_order,
):
    count = lax.axis_size("seq")
    place = lax.axis_index("seq")
    rows, heads, width = ssd_input.shape
    groups, size = input_map.shape[1:]
    per = heads // groups
    span = per * width
    q_rows, q_heads, q_width = queries.shape
    half = q_rows // 2

    kv = lax.all_gather(
        jnp.concatenate([key_rows, value_rows], axis=1), "seq", axis=0, tiled=True
    )

    chunk = min(4, per)
    chunks = heads // chunk
    per_chunks = per // chunk
    step = chunk * width
    decays = pair_decays(log_decay, chunks, width)
    x = ssd_input.reshape(rows, heads * width)
    dy = ssd_cotangent.reshape(rows, heads * width)
    a = log_decay.reshape(rows, groups, per).transpose(1, 0, 2)
    a_chunks = log_decay.reshape(rows, chunks, chunk).transpose(1, 0, 2)
    a_t = a_chunks.transpose(0, 2, 1)
    b = input_map.transpose(1, 0, 2)
    c = output_map.transpose(1, 0, 2)

    wide_spec = pl.BlockSpec((rows, span), lambda g: (0, g))
    a_spec = pl.BlockSpec((1, rows, per), lambda g: (g, 0, 0))
    map_spec = pl.BlockSpec((1, rows, size), lambda g: (g, 0, 0))
    state_flops = 4 * rows * heads * width * size
    sp = pl.pallas_call(
        state_kernel,
        grid=(groups,),
        in_specs=[wide_spec, wide_spec, a_spec, map_spec, map_spec],
        out_specs=pl.BlockSpec((per_chunks, 2, size, step), lambda g: (g, 0, 0, 0)),
        out_shape=jax.ShapeDtypeStruct((chunks, 2, size, step), BF16),
        scratch_shapes=[pltpu.VMEM((rows, span), BF16), pltpu.VMEM((rows, span), BF16)],
        compiler_params=pltpu.CompilerParams(vmem_limit_bytes=VMEM_BYTES),
        cost_estimate=pl.CostEstimate(
            flops=state_flops, bytes_accessed=4 * rows * heads * width, transcendentals=0
        ),
    )(x, dy, a, b, c)

    blocks = 2 * count
    own_first = pair_order[place]
    own = jnp.stack([own_first, blocks - 1 - own_first]).astype(jnp.int32)
    ids = jnp.stack([pair_order, blocks - 1 - pair_order], axis=1).reshape(-1)
    block_ids = jnp.arange(blocks, dtype=jnp.int32)
    where_at = jnp.sum(
        jnp.where(ids[None, :] == block_ids[:, None], block_ids[None, :], 0), axis=1
    ).astype(jnp.int32)

    def by_half(array):
        parts = array.reshape(2, half, q_heads, q_width).transpose(0, 2, 1, 3)
        return parts.reshape(2, q_heads * half, q_width)

    vmem = pl.BlockSpec(memory_space=pltpu.VMEM)
    smem = pl.BlockSpec(memory_space=pltpu.SMEM)
    quarters = lax.axis_size("head")
    lanes_q = q_heads * half
    dq, dkv = pl.pallas_call(
        attention_kernel,
        in_specs=[smem, smem, vmem, vmem, vmem],
        out_specs=[vmem, vmem],
        out_shape=[
            jax.ShapeDtypeStruct((2, lanes_q, q_width), BF16),
            jax.ShapeDtypeStruct((quarters, count, q_rows // quarters, 2 * q_width), BF16),
        ],
        scratch_shapes=[
            pltpu.VMEM((blocks, half, lanes_q), F32),
            pltpu.VMEM((blocks, half, lanes_q), BF16),
            pltpu.VMEM((count * q_rows, 2 * q_width), F32),
        ],
        compiler_params=pltpu.CompilerParams(vmem_limit_bytes=VMEM_BYTES),
        cost_estimate=pl.CostEstimate(
            flops=12 * (blocks + 1) * half * lanes_q * q_width,
            bytes_accessed=4 * count * q_rows * q_width * 4,
            transcendentals=(blocks + 1) * half * lanes_q,
        ),
    )(where_at, own, by_half(queries), by_half(attn_cotangent), kv)

    sp, dkv = lax.optimization_barrier((sp, dkv))
    dkv = lax.psum_scatter(dkv, "head", scatter_dimension=0, tiled=True)[0]
    dkv = lax.psum_scatter(dkv, "seq", scatter_dimension=0, tiled=True)[0]
    dkv = lax.all_gather(dkv, "head", axis=0, tiled=True)
    grad_keys = dkv[:, :q_width]
    grad_values = dkv[:, q_width:]
    grad_queries = (
        dq.reshape(2, q_heads, half, q_width).transpose(0, 2, 1, 3).reshape(queries.shape)
    )

    pairs = count // 2
    parts = rows // BLOCK
    sems = [pltpu.SemaphoreType.DMA((chunks,)) for _ in range(6)]
    dx, da, db, dc = pl.pallas_call(
        functools.partial(scan_kernel, pairs),
        in_specs=[vmem] * 8,
        out_specs=[vmem] * 4,
        out_shape=[
            jax.ShapeDtypeStruct((rows, heads * width), BF16),
            jax.ShapeDtypeStruct((chunks, rows, chunk), F32),
            jax.ShapeDtypeStruct((groups, rows, size), F32),
            jax.ShapeDtypeStruct((groups, rows, size), F32),
        ],
        scratch_shapes=[
            pltpu.VMEM((chunks, 2, size, step), BF16),
            pltpu.VMEM((chunks, size, step), BF16),
            pltpu.VMEM((chunks, size, step), BF16),
            pltpu.VMEM((chunks, size, step), BF16),
            pltpu.VMEM((chunks, size, step), BF16),
            pltpu.VMEM((parts, size, step), BF16),
            pltpu.VMEM((rows, step), BF16),
            pltpu.VMEM((chunks, size, step), F32),
            pltpu.VMEM((chunks, size, step), F32),
            pltpu.VMEM((groups * parts, BLOCK, BLOCK), F32),
            pltpu.VMEM((groups * parts, BLOCK, BLOCK), F32),
            pltpu.VMEM((groups * parts, 2, BLOCK, size), BF16),
            pltpu.VMEM((groups * parts, 2, size, BLOCK), BF16),
            *sems,
        ],
        compiler_params=pltpu.CompilerParams(
            vmem_limit_bytes=VMEM_BYTES, collective_id=0, has_side_effects=True
        ),
        cost_estimate=pl.CostEstimate(
            flops=5 * state_flops,
            bytes_accessed=8 * rows * heads * width,
            transcendentals=rows * heads * BLOCK,
        ),
    )(x, dy, a_chunks, a_t, b, c, sp, decays)

    return (
        dx.reshape(rows, heads, width),
        da.transpose(1, 0, 2).reshape(rows, heads),
        db.transpose(1, 0, 2),
        dc.transpose(1, 0, 2),
        grad_queries,
        grad_keys,
        grad_values,
    )


def solution(mesh):
    return jax.shard_map(
        per_device,
        mesh=mesh,
        in_specs=(
            P("seq", "head", None),
            P("seq", "head"),
            P("seq", "head", None),
            P("seq", "head", None),
            P("seq", "head", None),
            P("seq", "head", None),
            P("seq", None),
            P("seq", None),
            P("seq", "head", None),
            P(),
        ),
        out_specs=(
            P("seq", "head", None),
            P("seq", "head"),
            P("seq", "head", None),
            P("seq", "head", None),
            P("seq", "head", None),
            P("seq", None),
            P("seq", None),
        ),
        check_vma=False,
    )
```

time: 322 us -> 258 us (0.80)
  Pallas kernels: 65.9 us -> 126 us
  blocking collectives: 79.3 us -> 27.5 us
  waiting for transfers between devices: 94.5 us -> 52.3 us
  starting transfers between devices: 21.4 us -> 0.12 us
  other arithmetic: 17.3 us -> 3.97 us
  local copies, waits for them, and re-layouts: 28.6 us -> 33.1 us
    ppermute x7 -> x0, waiting for transfers between devices: 94.4 us -> none  [the longest x3 52.3 us: states_between(): ahead = lax.ppermute(ahead, 'seq', [(i, i + 2) for i in range(count - 2)])]
    all_gather x1 -> x0, blocking collectives: 73.3 us -> none  [states_between(): tots = lax.all_gather(tot[:, 0, :], 'seq')]
    pallas_call x1, Pallas kernels: 35 us -> 95.1 us  [per_device(): pl.pallas_call(functools.partial(scan_kernel, pairs), in_specs=[vmem] * 8...]
    reduce_scatter x1, waiting for transfers between devices: 0.01 us -> 30.1 us  [per_device(): dkv = lax.psum_scatter(dkv, 'head', scatter_dimension=0, tiled=True)[0]]
    all_gather x1, waiting for transfers between devices: 0.01 us -> 22.2 us  [per_device(): lax.all_gather(jnp.concatenate([key_rows, value_rows], axis=1), 'seq', ax...]
    unnamed x0 -> x1, blocking collectives: none -> 21.5 us
    ppermute x7 -> x0, starting transfers between devices: 21.3 us -> none  [the longest x3 14.5 us: states_between(): ahead = lax.ppermute(ahead, 'seq', [(i, i + 2) for i in range(count - 2)])]
    select_n x2 -> x0, other arithmetic: 9.96 us -> none  [the longest x1 5.69 us: states_between(): grad_in = jnp.where(odd == 1, p_sum, p_sum * decay_second + second_p)]
  transfers between devices with their start and end apart: 10 -> 3, of which waited for: 5 -> 2; matrix products, arithmetic and copies ran while one was open for 8% -> 13% of each run, Pallas kernels for 17% -> 41%
where the time goes in v2:
time: 258 us
  Pallas kernels  126 us (49%)
  waiting for transfers between devices  52.3 us (20%)
  local copies, waits for them, and re-layouts  33.1 us (13%)
  blocking collectives  27.5 us (11%)
  between operations  15.2 us (6%)
  other arithmetic  3.97 us (2%)
    pallas_call x1, Pallas kernels, per_device(): pl.pallas_call(functools.partial(scan_kernel, pairs), in_specs=[vmem] * 8...  95.1 us
    reduce_scatter x1, waiting for transfers between devices, per_device(): dkv = lax.psum_scatter(dkv, 'head', scatter_dimension=0, tiled=True)[0]  30.1 us
    all_gather x1, waiting for transfers between devices, per_device(): lax.all_gather(jnp.concatenate([key_rows, value_rows], axis=1), 'seq', ax...  22.2 us
    unnamed x1, blocking collectives  21.5 us
    pallas_call x1, Pallas kernels, per_device(): pl.pallas_call(attention_kernel, in_specs=[smem, smem, vmem, vmem, vmem],...  20.9 us
    reshape x1, local copies, waits for them, and re-layouts, per_device(): dy = ssd_cotangent.reshape(rows, heads * width)  13.4 us
    pallas_call x1, Pallas kernels, per_device(): pl.pallas_call(state_kernel, grid=(groups,), in_specs=[wide_spec, wide_sp...  9.62 us
    unnamed x14, local copies, waits for them, and re-layouts  8.87 us
  transfers between devices with their start and end apart: 3, of which 2 were waited for; matrix products, arithmetic and copies ran while one was open for 13% of the time, Pallas kernels for 41%

profile of v2, /device:TPU:0, one launch (start us, length us, event | category | flops | bytes accessed | tf_op | source)
XLA Modules:
  0.0 257.8 jit_solution(5540043630466240799)
XLA Ops:
  7.2 1.7 pad_maximum_fusion
  9.0 1.2 dynamic_slice.6
  10.2 0.7 subtract_bitcast_fusion
  10.9 0.7 pad_add_fusion
  11.7 1.0 copy.42
  12.7 1.0 copy.43
  13.7 1.0 copy.40
  15.4 1.3 copy_bitcast_fusion.2
  16.7 13.4 %copy_bitcast_fusion = (bf16[512,4096]{1,0:T(8,128)(2,1)}, bf16[512,4096]{1,0:T(8,128)(2,1)}) fusion(bf16[64,8,32,128]{3,2,1,0:T(8,128)(2,1)} %bitcast.57, bf16[64,8,32,128]{3,2,1,0:T(8,128)(2,1)} %bitcast.58), kind=kLoop, calls=%fused_computation | loop fusion | bytes 16777216 | tf_op jit(solution)/shard_map/reshape | solution.py:475
  30.1 9.6 %shard_map.153.sp_ref = bf16[8,2,128,512]{3,2,1,0:T(8,128)(2,1)} custom-call(bf16[512,4096]{1,0:T(8,128)(2,1)} %get-tuple-element.47.x_ref, bf16[512,4096]{1,0:T(8,128)(2,1)} %get-tuple-element.46.dy_ref, f32[2,512,16]{2,1,0:T(8,128)S(1)} %bitcast.46, f32[2,512,128]{2,1,0:T(8,128)S(1)} %get-tuple-element.49.b_ref, f32[2,512,128]{2,1,0:T(8,128)S(1)} %get-tuple-element.48.c_ref), custom_call_target="tpu_custom_call" | custom-call | flops 1073741824 | bytes 8388608 | tf_op jit(solution)/shard_map/pallas_call | solution.py:486
  39.7 0.7 pad_add_fusion.1.own_ref
  40.6 22.2 %all-gather.4.cloned.1.call-done.kv_ref = bf16[4096,256]{1,0:T(8,128)(2,1)} async-done(((bf16[512,256]{1,0:T(8,128)(2,1)}), bf16[4096,256]{1,0:T(8,128)(2,1)}) %all-gather.4.cloned.1.call-update) | async-done | bytes 2097168 | tf_op jit(solution)/shard_map/all_gather | solution.py:465
  62.7 20.9 %shard_map.154 = (bf16[2,512,128]{2,1,0:T(8,128)(2,1)S(1)}, bf16[4,8,128,256]{3,2,1,0:T(8,128)(2,1)}) custom-call(s32[16]{0:T(128)S(1)} %select_reduce_fusion.place_ref, s32[2]{0:T(128)S(1)} %pad_add_fusion.1.own_ref, bf16[2,512,128]{2,1,0:T(8,128)(2,1)S(1)} %bitcast.52, bf16[2,512,128]{2,1,0:T(8,128)(2,1)S(1)} %bitcast.53, ...), custom_call_target="tpu_custom_call" | custom-call | flops 3422552064 | bytes 8388608 | tf_op jit(solution)/shard_map/pallas_call | solution.py:516
  83.7 30.1 %reduce-scatter.3.cloned.1.call-done = bf16[1,8,128,256]{3,2,1,0:T(8,128)(2,1)} async-done(((bf16[4,8,128,256]{3,2,1,0:T(8,128)(2,1)}), bf16[1,8,128,256]{3,2,1,0:T(8,128)(2,1)}) %reduce-scatter.3.cloned.1.call-update) | async-done | bytes 524304 | tf_op jit(solution)/shard_map/reduce_scatter | solution.py:538
  115.5 21.5 %all-reduce.1 = f32[8,1,32]{2,0,1:T(8,128)S(1)} all-reduce(f32[8,1,32]{2,0,1:T(8,128)S(1)} %reshape.68), channel_id=2, replica_groups=mesh['seq'=8,'head'=4] {'seq'}, use_global_device_ids=true, to_apply=%add | all-reduce | flops 256 | bytes 2048
  137.2 2.0 copy.45.a_ref
  139.2 1.0 copy.47
  140.1 95.1 %shard_map.155 = (bf16[512,4096]{1,0:T(8,128)(2,1)}, f32[8,512,4]{2,1,0:T(8,128)}, f32[2,512,128]{2,1,0:T(8,128)S(1)}, f32[2,512,128]{2,1,0:T(8,128)S(1)}) custom-call(bf16[512,4096]{1,0:T(8,128)(2,1)} %get-tuple-element.47.x_ref, bf16[512,4096]{1,0:T(8,128)(2,1)} %get-tuple-element.46.dy_ref, f32[8,512,4]{2,1,0:T(8,128)} %copy.45.a_ref, ...), custom_call_target="tpu_custom_call" | custom-call | flops 5368709120 | bytes 16777216 | tf_op jit(solution)/shard_map/pallas_call | solution.py:550
  235.2 5.6 %copy.52 = bf16[64,8,32,128]{3,2,1,0:T(8,128)(2,1)} copy(bf16[64,8,32,128]{3,1,2,0:T(8,128)(2,1)} %bitcast.56) | data formatting | bytes 8388608
  241.5 0.7 reshape.65
  242.2 1.2 copy.48
  243.4 1.2 copy.49
  244.6 6.0 %all-gather.1 = bf16[1,512,256]{2,1,0:T(8,128)(2,1)S(1)} all-gather(bf16[1,128,256]{2,1,0:T(8,128)(2,1)} %reduce-scatter.5.cloned.1.call-done), channel_id=3, replica_groups=mesh['seq'=8,'head'=4] {'head'}, dimensions={1}, use_global_device_ids=true | all-gather | bytes 327680 | tf_op jit(solution)/shard_map/all_gather | solution.py:540
  250.5 0.7 fusion
  (29 shorter events, 2.3 us)
Async XLA Ops:
  7.2 55.6 %all-gather.4.cloned.1.call-start = ((), (), s32[]{:S(2)}) async-start(), calls=%async_computation.2 | async-start | bytes 2359296 | tf_op jit(solution)/shard_map/all_gather | solution.py:465
  8.9 104.8 %reduce-scatter.3.cloned.1.call-start = ((), (), s32[]{:S(2)}) async-start(), calls=%async_computation.3 | async-start | bytes 2621440 | tf_op jit(solution)/shard_map/reduce_scatter | solution.py:538
  16.7 13.4 %copy-start = (f32[2,512,128]{2,1,0:T(8,128)}, f32[2,512,128]{2,1,0:T(8,128)S(1)}, u32[]{:S(2)}) copy-start(f32[2,512,128]{2,1,0:T(8,128)S(1)} %get-tuple-element.48.c_ref) | copy-start | bytes 1572868
  62.7 51.1 %copy-start.2 = (f32[512,32]{0,1:T(8,128)S(1)}, f32[512,32]{0,1:T(8,128)}, u32[]{:S(2)}) copy-start(f32[512,32]{0,1:T(8,128)} %param.11) | copy-start | bytes 196612
  62.7 51.2 %copy-start.3 = (u32[32]{0:T(128)S(1)}, u32[32]{0:T(128)}, u32[]{:S(2)}) copy-start(u32[32]{0:T(128)} %constant.38) | copy-start | bytes 388
  83.6 160.9 %reduce-scatter.5.cloned.1.call-start = ((), (), s32[]{:S(2)}) async-start(), calls=%async_computation.4 | async-start | bytes 589824 | tf_op jit(solution)/shard_map/reduce_scatter | solution.py:539
  235.2 5.6 %copy-start.1 = (f32[8,512,4]{2,1,0:T(8,128)S(1)}, f32[8,512,4]{2,1,0:T(8,128)}, u32[]{:S(2)}) copy-start(f32[8,512,4]{2,1,0:T(8,128)} %get-tuple-element.18) | copy-start | bytes 196612
Sparse Core Ops, SparseCore 0:
  10.7 51.9 all-gather.3
  83.8 29.9 reduce-scatter.2
  117.5 62.5 reduce-scatter.4

commit v3 on v2

--- a/solution.py
+++ b/solution.py
@@ -98,6 +98,8 @@
     dgt,
     maps_low,
     maps_t,
+    cums,
+    cums_t,
     y_send,
     y_recv,
     f_send,
@@ -105,7 +107,9 @@
     b_send,
     b_recv,
 ):
-    chunks, rows, heads = a_ref.shape
+    chunks = sp_ref.shape[0]
+    rows, all_heads = a_ref.shape
+    heads = all_heads // chunks
     groups, _, size = b_ref.shape
     per_group = chunks // groups
     width = x_ref.shape[1] // (chunks * heads)
@@ -160,6 +164,14 @@
     db_ref[...] = jnp.zeros_like(db_ref)
     dc_ref[...] = jnp.zeros_like(dc_ref)
     dgt[...] = jnp.zeros_like(dgt)
+    da_ref[...] = jnp.zeros_like(da_ref)
+    for k in range(count):
+        span = pl.ds(k * BLOCK, BLOCK)
+        cum = dot_hi(lower, a_ref[span, :])
+        cum_t = dot_hi(at_ref[:, span], upper)
+        for c in range(chunks):
+            cums[c, span, :] = cum[:, c * heads : (c + 1) * heads]
+            cums_t[c, :, span] = cum_t[c * heads : (c + 1) * heads, :]
 
     def prepare(at, carry):
         g = at // count
@@ -227,7 +239,7 @@
 
         def forward(k, carry):
             span = pl.ds(pl.multiple_of(k * BLOCK, BLOCK), BLOCK)
-            cum = dot_hi(lower, a_ref[c, span, :])
+            cum = cums[c, span, :]
             last = cum[BLOCK - 1 :, :]
             tail = jnp.exp(last - cum)
             whole = jnp.exp(last)
@@ -247,8 +259,8 @@
             k = count - 1 - turn
             at = g * count + k
             span = pl.ds(pl.multiple_of(k * BLOCK, BLOCK), BLOCK)
-            cum = dot_hi(lower, a_ref[c, span, :])
-            cum_t = dot_hi(at_ref[c, :, span], upper)
+            cum = cums[c, span, :]
+            cum_t = cums_t[c, :, span]
             last = cum[BLOCK - 1 :, :]
             tail = jnp.exp(last - cum)
             whole = jnp.exp(last)
@@ -257,11 +269,11 @@
             c_low = maps_low[at, 1]
             c_t = maps_t[at, 1]
             gt = gts[at]
-            columns = jnp.zeros((BLOCK, heads), F32)
-            row_sums = jnp.zeros((heads, BLOCK), F32)
-            totals = jnp.zeros((heads, BLOCK), F32)
-            column_at = iota2((BLOCK, heads), 1)
-            row_at = iota2((heads, BLOCK), 0)
+            columns = jnp.zeros((BLOCK, all_heads), F32)
+            row_sums = jnp.zeros((all_heads, BLOCK), F32)
+            totals = jnp.zeros((all_heads, BLOCK), F32)
+            column_at = iota2((BLOCK, all_heads), 1) - c * heads
+            row_at = iota2((all_heads, BLOCK), 0) - c * heads
             db = jnp.zeros((BLOCK, size), F32)
             dc = jnp.zeros((BLOCK, size), F32)
             dg = jnp.zeros((BLOCK, BLOCK), F32)
@@ -300,8 +312,10 @@
             db_ref[g, span, :] += db
             dc_ref[g, span, :] += dc
             total = jnp.sum(totals, axis=1, keepdims=True)
-            row_sums = row_sums + jnp.where(iota2((heads, BLOCK), 1) == BLOCK - 1, total, 0.0)
-            da_ref[c, span, :] = dot_hi(upper, columns + row_sums.T)
+            row_sums = row_sums + jnp.where(
+                iota2((all_heads, BLOCK), 1) == BLOCK - 1, total, 0.0
+            )
+            da_ref[span, :] += columns + row_sums.T
             return carry
 
         lax.fori_loop(0, count, backward, 0)
@@ -346,6 +360,10 @@
         return carry
 
     lax.fori_loop(0, groups * count, finish, 0)
+
+    for k in range(count):
+        span = pl.ds(k * BLOCK, BLOCK)
+        da_ref[span, :] = dot_hi(upper, da_ref[span, :])
 
     def settle(c, carry):
         swap(c).wait_send()
@@ -434,10 +452,13 @@
 
 
 def pair_decays(log_decay, chunks, width):
-    pair = lax.axis_index("seq") // 2
-    tots = lax.all_gather(jnp.sum(log_decay, axis=0, keepdims=True), "seq")
-    own = lax.dynamic_slice_in_dim(tots[:, 0], 2 * pair, 2, 0)
-    decays = jnp.repeat(jnp.exp(own), width, axis=1)
+    count = lax.axis_size("seq")
+    is_odd = lax.axis_index("seq") % 2 == 1
+    own = jnp.sum(log_decay, axis=0, keepdims=True)
+    other = lax.ppermute(own, "seq", [(i, i ^ 1) for i in range(count)])
+    first = jnp.where(is_odd, other, own)
+    second = jnp.where(is_odd, own, other)
+    decays = jnp.repeat(jnp.exp(jnp.concatenate([first, second])), width, axis=1)
     return decays.reshape(2, chunks, -1).transpose(1, 0, 2)
 
 
@@ -462,9 +483,12 @@
     q_rows, q_heads, q_width = queries.shape
     half = q_rows // 2
 
-    kv = lax.all_gather(
-        jnp.concatenate([key_rows, value_rows], axis=1), "seq", axis=0, tiled=True
-    )
+    quarters = lax.axis_size("head")
+    share = q_rows // quarters
+    kv = jnp.concatenate([key_rows, value_rows], axis=1)
+    kv = lax.dynamic_slice_in_dim(kv, lax.axis_index("head") * share, share, 0)
+    kv = lax.all_gather(lax.all_gather(kv, "seq"), "head", axis=1, tiled=True)
+    kv = kv.reshape(count * q_rows, 2 * q_width)
 
     chunk = min(4, per)
     chunks = heads // chunk
@@ -474,8 +498,7 @@
     x = ssd_input.reshape(rows, heads * width)
     dy = ssd_cotangent.reshape(rows, heads * width)
     a = log_decay.reshape(rows, groups, per).transpose(1, 0, 2)
-    a_chunks = log_decay.reshape(rows, chunks, chunk).transpose(1, 0, 2)
-    a_t = a_chunks.transpose(0, 2, 1)
+    a_t = log_decay.T
     b = input_map.transpose(1, 0, 2)
     c = output_map.transpose(1, 0, 2)
 
@@ -511,7 +534,6 @@
 
     vmem = pl.BlockSpec(memory_space=pltpu.VMEM)
     smem = pl.BlockSpec(memory_space=pltpu.SMEM)
-    quarters = lax.axis_size("head")
     lanes_q = q_heads * half
     dq, dkv = pl.pallas_call(
         attention_kernel,
@@ -535,8 +557,8 @@
     )(where_at, own, by_half(queries), by_half(attn_cotangent), kv)
 
     sp, dkv = lax.optimization_barrier((sp, dkv))
-    dkv = lax.psum_scatter(dkv, "head", scatter_dimension=0, tiled=True)[0]
-    dkv = lax.psum_scatter(dkv, "seq", scatter_dimension=0, tiled=True)[0]
+    dkv = dkv.reshape(quarters * count * share, 2 * q_width)
+    dkv = lax.psum_scatter(dkv, ("head", "seq"), scatter_dimension=0, tiled=True)
     dkv = lax.all_gather(dkv, "head", axis=0, tiled=True)
     grad_keys = dkv[:, :q_width]
     grad_values = dkv[:, q_width:]
@@ -553,7 +575,7 @@
         out_specs=[vmem] * 4,
         out_shape=[
             jax.ShapeDtypeStruct((rows, heads * width), BF16),
-            jax.ShapeDtypeStruct((chunks, rows, chunk), F32),
+            jax.ShapeDtypeStruct((rows, heads), F32),
             jax.ShapeDtypeStruct((groups, rows, size), F32),
             jax.ShapeDtypeStruct((groups, rows, size), F32),
         ],
@@ -571,6 +593,8 @@
             pltpu.VMEM((groups * parts, BLOCK, BLOCK), F32),
             pltpu.VMEM((groups * parts, 2, BLOCK, size), BF16),
             pltpu.VMEM((groups * parts, 2, size, BLOCK), BF16),
+            pltpu.VMEM((chunks, rows, chunk), F32),
+            pltpu.VMEM((chunks, chunk, rows), F32),
             *sems,
         ],
         compiler_params=pltpu.CompilerParams(
@@ -581,11 +605,11 @@
             bytes_accessed=8 * rows * heads * width,
             transcendentals=rows * heads * BLOCK,
         ),
-    )(x, dy, a_chunks, a_t, b, c, sp, decays)
+    )(x, dy, log_decay, a_t, b, c, sp, decays)
 
     return (
         dx.reshape(rows, heads, width),
-        da.transpose(1, 0, 2).reshape(rows, heads),
+        da,
         db.transpose(1, 0, 2),
         dc.transpose(1, 0, 2),
         grad_queries,

time: 258 us -> 251 us (0.973)
  waiting for transfers between devices: 52.3 us -> 35.8 us
  blocking collectives: 27.5 us -> 41.2 us
  Pallas kernels: 126 us -> 123 us
  local copies, waits for them, and re-layouts: 33.1 us -> 30.2 us
    all_gather x0 -> x1, blocking collectives: none -> 35.2 us  [per_device(): kv = lax.all_gather(lax.all_gather(kv, 'seq'), 'head', axis=1, tiled=True)]
    all_gather x1, waiting for transfers between devices: 22.2 us -> 0.01 us  [per_device(): kv = lax.all_gather(lax.all_gather(kv, 'seq'), 'head', axis=1, tiled=True)]
    unnamed x1 -> x0, blocking collectives: 21.5 us -> none
    reduce_scatter x2 -> x1, waiting for transfers between devices: 30.1 us -> 34.1 us  [per_device(): lax.psum_scatter(dkv, ('head', 'seq'), scatter_dimension=0, tiled=True)]
    transpose x2 -> x0, local copies, waits for them, and re-layouts: 2.58 us -> none  [the longest x1 1.96 us: per_device(): a_chunks = log_decay.reshape(rows, chunks, chunk).transpose(1, 0, 2)]
    unnamed x14 -> x11, local copies, waits for them, and re-layouts: 8.87 us -> 8.77 us
where the time goes in v3:
time: 251 us; the launch traced here: 250 us
  Pallas kernels  123 us (49%)
  blocking collectives  41.2 us (16%)
  waiting for transfers between devices  35.8 us (14%)
  local copies, waits for them, and re-layouts  30.2 us (12%)
  between operations  14.8 us (6%)
  other arithmetic  3.07 us (1%)
    pallas_call x1, Pallas kernels, per_device(): pl.pallas_call(functools.partial(scan_kernel, pairs), in_specs=[vmem] * 8...  92.9 us
    all_gather x1, blocking collectives, per_device(): kv = lax.all_gather(lax.all_gather(kv, 'seq'), 'head', axis=1, tiled=True)  35.2 us
    reduce_scatter x1, waiting for transfers between devices, per_device(): lax.psum_scatter(dkv, ('head', 'seq'), scatter_dimension=0, tiled=True)  34.1 us
    pallas_call x1, Pallas kernels, per_device(): pl.pallas_call(attention_kernel, in_specs=[smem, smem, vmem, vmem, vmem],...  20.8 us
    reshape x1, local copies, waits for them, and re-layouts, per_device(): dy = ssd_cotangent.reshape(rows, heads * width)  13.9 us
    pallas_call x1, Pallas kernels, per_device(): pl.pallas_call(state_kernel, grid=(groups,), in_specs=[wide_spec, wide_sp...  9.64 us
    unnamed x11, local copies, waits for them, and re-layouts  8.77 us
    all_gather x1, blocking collectives, per_device(): dkv = lax.all_gather(dkv, 'head', axis=0, tiled=True)  5.98 us
  transfers between devices with their start and end apart: 3, of which 2 were waited for; matrix products, arithmetic and copies ran while one was open for 13% of the time, Pallas kernels for 41%

profile of v3, /device:TPU:0, one launch (start us, length us, event | category | flops | bytes accessed | tf_op | source)
XLA Modules:
  0.0 250.4 jit_solution(14990988622276623206)
XLA Ops:
  7.2 0.8 fusion
  8.0 35.2 %all-gather = bf16[1024,256]{1,0:T(8,128)(2,1)} all-gather(bf16[128,256]{1,0:T(8,128)(2,1)S(1)} %fusion), channel_id=2, replica_groups=mesh['seq'=8,'head'=4] {'seq'}, dimensions={0}, use_global_device_ids=true | all-gather | bytes 589824 | tf_op jit(solution)/shard_map/all_gather | solution.py:490
  43.3 1.2 dynamic_slice.6
  44.6 0.7 subtract_bitcast_fusion
  45.2 0.7 pad_add_fusion
  46.0 1.0 copy.43
  47.0 1.0 copy.44
  48.0 1.0 copy.41
  49.7 1.3 copy_bitcast_fusion.2
  51.1 13.9 %copy_bitcast_fusion = (bf16[512,4096]{1,0:T(8,128)(2,1)}, bf16[512,4096]{1,0:T(8,128)(2,1)}) fusion(bf16[64,8,32,128]{3,2,1,0:T(8,128)(2,1)} %bitcast.52, bf16[64,8,32,128]{3,2,1,0:T(8,128)(2,1)} %bitcast.53), kind=kLoop, calls=%fused_computation | loop fusion | bytes 16777216 | tf_op jit(solution)/shard_map/reshape | solution.py:499
  65.0 9.6 %shard_map.153.sp_ref = bf16[8,2,128,512]{3,2,1,0:T(8,128)(2,1)} custom-call(bf16[512,4096]{1,0:T(8,128)(2,1)} %get-tuple-element.49.x_ref, bf16[512,4096]{1,0:T(8,128)(2,1)} %get-tuple-element.48.dy_ref, f32[2,512,16]{2,1,0:T(8,128)S(1)} %bitcast.41, f32[2,512,128]{2,1,0:T(8,128)S(1)} %get-tuple-element.51.b_ref, f32[2,512,128]{2,1,0:T(8,128)S(1)} %get-tuple-element.50.c_ref), custom_call_target="tpu_custom_call" | custom-call | flops 1073741824 | bytes 8388608 | tf_op jit(solution)/shard_map/pallas_call | solution.py:509
  74.6 0.7 pad_add_fusion.1.own_ref
  75.5 20.8 %shard_map.154 = (bf16[2,512,128]{2,1,0:T(8,128)(2,1)S(1)}, bf16[4,8,128,256]{3,2,1,0:T(8,128)(2,1)}) custom-call(s32[16]{0:T(128)S(1)} %select_reduce_fusion.place_ref, s32[2]{0:T(128)S(1)} %pad_add_fusion.1.own_ref, bf16[2,512,128]{2,1,0:T(8,128)(2,1)S(1)} %bitcast.47, bf16[2,512,128]{2,1,0:T(8,128)(2,1)S(1)} %bitcast.48, bf16[4096,256]{1,0:T(8,128)(2,1)} %bitcast.61), custom_call_target="tpu_custom_call" | custom-call | flops 3422552064 | bytes 8388608 | tf_op jit(solution)/shard_map/pallas_call | solution.py:538
  96.5 1.8 collective-permute-start
  98.5 1.6 collective-permute-done
  100.2 1.0 copy.47
  101.2 92.9 %shard_map.155 = (bf16[512,4096]{1,0:T(8,128)(2,1)}, f32[512,32]{1,0:T(8,128)S(1)}, f32[2,512,128]{2,1,0:T(8,128)S(1)}, f32[2,512,128]{2,1,0:T(8,128)S(1)}) custom-call(bf16[512,4096]{1,0:T(8,128)(2,1)} %get-tuple-element.49.x_ref, bf16[512,4096]{1,0:T(8,128)(2,1)} %get-tuple-element.48.dy_ref, f32[512,32]{1,0:T(8,128)S(1)} %copy.46.a_ref, ...), custom_call_target="tpu_custom_call" | custom-call | flops 5368709120 | bytes 16777216 | tf_op jit(solution)/shard_map/pallas_call | solution.py:572
  194.1 5.5 %copy.53 = bf16[64,8,32,128]{3,2,1,0:T(8,128)(2,1)} copy(bf16[64,8,32,128]{3,1,2,0:T(8,128)(2,1)} %bitcast.51) | data formatting | bytes 8388608
  199.6 0.7 copy.48
  200.3 1.2 copy.49
  201.5 1.2 copy.50
  202.7 34.1 %reduce-scatter.2.cloned.1.call-done = bf16[128,256]{1,0:T(8,128)(2,1)} async-done(((bf16[4096,256]{1,0:T(8,128)(2,1)}), bf16[128,256]{1,0:T(8,128)(2,1)}) %reduce-scatter.2.cloned.1.call-update) | async-done | bytes 65552 | tf_op jit(solution)/shard_map/reduce_scatter | solution.py:561
  236.9 6.0 %all_gather.15 = bf16[512,256]{1,0:T(8,128)(2,1)S(1)} all-gather(bf16[128,256]{1,0:T(8,128)(2,1)} %reduce-scatter.2.cloned.1.call-done), channel_id=1, replica_groups=mesh['seq'=8,'head'=4] {'head'}, dimensions={0}, use_global_device_ids=true | all-gather | bytes 327680 | tf_op jit(solution)/shard_map/all_gather | solution.py:562
  242.9 0.7 fusion.1
  (21 shorter events, 0.8 us)
Async XLA Ops:
  7.2 68.3 %all-gather.3.cloned.1.call-start = ((), (), s32[]{:S(2)}) async-start(), calls=%async_computation.1 | async-start | bytes 2621440 | tf_op jit(solution)/shard_map/all_gather | solution.py:490
  43.3 193.6 %reduce-scatter.2.cloned.1.call-start = ((), (), s32[]{:S(2)}) async-start(), calls=%async_computation.2 | async-start | bytes 2162688 | tf_op jit(solution)/shard_map/reduce_scatter | solution.py:561
  51.1 13.9 %copy-start = (f32[2,512,128]{2,1,0:T(8,128)}, f32[2,512,128]{2,1,0:T(8,128)S(1)}, u32[]{:S(2)}) copy-start(f32[2,512,128]{2,1,0:T(8,128)S(1)} %get-tuple-element.50.c_ref) | copy-start | bytes 1572868
  51.1 13.9 %copy-start.1 = (f32[2,512,128]{2,1,0:T(8,128)}, f32[2,512,128]{2,1,0:T(8,128)S(1)}, u32[]{:S(2)}) copy-start(f32[2,512,128]{2,1,0:T(8,128)S(1)} %get-tuple-element.51.b_ref) | copy-start | bytes 1572868
  75.5 20.9 %copy-start.2 = (f32[512,32]{0,1:T(8,128)S(1)}, f32[512,32]{0,1:T(8,128)}, u32[]{:S(2)}) copy-start(f32[512,32]{0,1:T(8,128)} %param.11) | copy-start | bytes 196612
  96.5 3.6 %collective-permute-start = (f32[1,32]{1,0:T(1,128)S(1)}, f32[1,32]{1,0:T(1,128)S(1)}, u32[]{:S(2)}, u32[]{:S(2)}) collective-permute-start(f32[1,32]{1,0:T(1,128)S(1)} %bitcast.59), channel_id=1, source_target_pairs={{0,4},{4,0},{8,12},{12,8},{16,20},{20,16},{24,28},{28,24},{1,5},{5... | collective-permute-start | bytes 392 | tf_op jit(solution)/shard_map/ppermute | solution.py:458
Sparse Core Ops, SparseCore 0:
  43.4 23.5 all-gather.2
  96.5 140.3 reduce-scatter.1

commit v4 on v3

--- a/solution.py
+++ b/solution.py
@@ -484,11 +484,9 @@
     half = q_rows // 2
 
     quarters = lax.axis_size("head")
-    share = q_rows // quarters
-    kv = jnp.concatenate([key_rows, value_rows], axis=1)
-    kv = lax.dynamic_slice_in_dim(kv, lax.axis_index("head") * share, share, 0)
-    kv = lax.all_gather(lax.all_gather(kv, "seq"), "head", axis=1, tiled=True)
-    kv = kv.reshape(count * q_rows, 2 * q_width)
+    kv = lax.all_gather(
+        jnp.concatenate([key_rows, value_rows], axis=1), "seq", axis=0, tiled=True
+    )
 
     chunk = min(4, per)
     chunks = heads // chunk
@@ -557,8 +555,8 @@
     )(where_at, own, by_half(queries), by_half(attn_cotangent), kv)
 
     sp, dkv = lax.optimization_barrier((sp, dkv))
-    dkv = dkv.reshape(quarters * count * share, 2 * q_width)
-    dkv = lax.psum_scatter(dkv, ("head", "seq"), scatter_dimension=0, tiled=True)
+    dkv = lax.psum_scatter(dkv, "head", scatter_dimension=0, tiled=True)[0]
+    dkv = lax.psum_scatter(dkv, "seq", scatter_dimension=0, tiled=True)[0]
     dkv = lax.all_gather(dkv, "head", axis=0, tiled=True)
     grad_keys = dkv[:, :q_width]
     grad_values = dkv[:, q_width:]

time: 251 us -> 222 us (0.88)
  blocking collectives: 41.2 us -> 5.98 us
  waiting for transfers between devices: 35.8 us -> 54 us
  Pallas kernels: 123 us -> 112 us
    all_gather x1 -> x0, blocking collectives: 35.2 us -> none  [per_device(): kv = lax.all_gather(lax.all_gather(kv, 'seq'), 'head', axis=1, tiled=True)]
    all_gather x1, waiting for transfers between devices: 0.01 us -> 22 us  [per_device(): lax.all_gather(jnp.concatenate([key_rows, value_rows], axis=1), 'seq', ax...]
    pallas_call x1, Pallas kernels: 92.9 us -> 81.5 us  [per_device(): pl.pallas_call(functools.partial(scan_kernel, pairs), in_specs=[vmem] * 8...]
    reduce_scatter x1 -> x2, waiting for transfers between devices: 34.1 us -> 30 us  [the longest x1 30 us: per_device(): dkv = lax.psum_scatter(dkv, 'head', scatter_dimension=0, tiled=True)[0]]
  transfers between devices with their start and end apart: 3 -> 4, of which waited for: 2 -> 3; matrix products, arithmetic and copies ran while one was open for 13% -> 14% of each run, Pallas kernels for 41% -> 41%
where the time goes in v4:
time: 222 us
  Pallas kernels  112 us (50%)
  waiting for transfers between devices  54 us (24%)
  local copies, waits for them, and re-layouts  29.8 us (13%)
  between operations  14.5 us (7%)
  blocking collectives  5.98 us (3%)
  other arithmetic  3.99 us (2%)
    pallas_call x1, Pallas kernels, per_device(): pl.pallas_call(functools.partial(scan_kernel, pairs), in_specs=[vmem] * 8...  81.5 us
    reduce_scatter x1, waiting for transfers between devices, per_device(): dkv = lax.psum_scatter(dkv, 'head', scatter_dimension=0, tiled=True)[0]  30 us
    all_gather x1, waiting for transfers between devices, per_device(): lax.all_gather(jnp.concatenate([key_rows, value_rows], axis=1), 'seq', ax...  22 us
    pallas_call x1, Pallas kernels, per_device(): pl.pallas_call(attention_kernel, in_specs=[smem, smem, vmem, vmem, vmem],...  21 us
    reshape x1, local copies, waits for them, and re-layouts, per_device(): dy = ssd_cotangent.reshape(rows, heads * width)  13.6 us
    pallas_call x1, Pallas kernels, per_device(): pl.pallas_call(state_kernel, grid=(groups,), in_specs=[wide_spec, wide_sp...  9.63 us
    unnamed x11, local copies, waits for them, and re-layouts  8.75 us
    all_gather x1, blocking collectives, per_device(): dkv = lax.all_gather(dkv, 'head', axis=0, tiled=True)  5.98 us
  transfers between devices with their start and end apart: 4, of which 3 were waited for; matrix products, arithmetic and copies ran while one was open for 14% of the time, Pallas kernels for 41%

profile of v4, /device:TPU:0, one launch (start us, length us, event | category | flops | bytes accessed | tf_op | source)
XLA Modules:
  0.0 222.1 jit_solution(1400336602876145532)
XLA Ops:
  7.2 1.7 pad_maximum_fusion
  9.0 1.2 dynamic_slice.3
  10.2 0.7 subtract_bitcast_fusion
  10.9 0.7 pad_add_fusion
  11.7 1.0 copy.43
  12.7 1.0 copy.44
  13.7 1.0 copy.41
  15.4 1.3 copy_bitcast_fusion.2
  16.7 13.6 %copy_bitcast_fusion = (bf16[512,4096]{1,0:T(8,128)(2,1)}, bf16[512,4096]{1,0:T(8,128)(2,1)}) fusion(bf16[64,8,32,128]{3,2,1,0:T(8,128)(2,1)} %bitcast.51, bf16[64,8,32,128]{3,2,1,0:T(8,128)(2,1)} %bitcast.52), kind=kLoop, calls=%fused_computation | loop fusion | bytes 16777216 | tf_op jit(solution)/shard_map/reshape | solution.py:497
  30.3 9.6 %shard_map.153.sp_ref = bf16[8,2,128,512]{3,2,1,0:T(8,128)(2,1)} custom-call(bf16[512,4096]{1,0:T(8,128)(2,1)} %get-tuple-element.49.x_ref, bf16[512,4096]{1,0:T(8,128)(2,1)} %get-tuple-element.48.dy_ref, f32[2,512,16]{2,1,0:T(8,128)S(1)} %bitcast.40, f32[2,512,128]{2,1,0:T(8,128)S(1)} %get-tuple-element.51.b_ref, f32[2,512,128]{2,1,0:T(8,128)S(1)} %get-tuple-element.50.c_ref), custom_call_target="tpu_custom_call" | custom-call | flops 1073741824 | bytes 8388608 | tf_op jit(solution)/shard_map/pallas_call | solution.py:507
  39.9 0.7 pad_add_fusion.1.own_ref
  40.7 22.0 %all-gather.3.cloned.1.call-done.kv_ref = bf16[4096,256]{1,0:T(8,128)(2,1)} async-done(((bf16[512,256]{1,0:T(8,128)(2,1)}), bf16[4096,256]{1,0:T(8,128)(2,1)}) %all-gather.3.cloned.1.call-update) | async-done | bytes 2097168 | tf_op jit(solution)/shard_map/all_gather | solution.py:487
  62.7 21.0 %shard_map.154 = (bf16[2,512,128]{2,1,0:T(8,128)(2,1)S(1)}, bf16[4,8,128,256]{3,2,1,0:T(8,128)(2,1)}) custom-call(s32[16]{0:T(128)S(1)} %select_reduce_fusion.place_ref, s32[2]{0:T(128)S(1)} %pad_add_fusion.1.own_ref, bf16[2,512,128]{2,1,0:T(8,128)(2,1)S(1)} %bitcast.46, bf16[2,512,128]{2,1,0:T(8,128)(2,1)S(1)} %bitcast.47, ...), custom_call_target="tpu_custom_call" | custom-call | flops 3422552064 | bytes 8388608 | tf_op jit(solution)/shard_map/pallas_call | solution.py:536
  83.8 30.0 %reduce-scatter.3.cloned.1.call-done = bf16[1,8,128,256]{3,2,1,0:T(8,128)(2,1)} async-done(((bf16[4,8,128,256]{3,2,1,0:T(8,128)(2,1)}), bf16[1,8,128,256]{3,2,1,0:T(8,128)(2,1)}) %reduce-scatter.3.cloned.1.call-update) | async-done | bytes 524304 | tf_op jit(solution)/shard_map/reduce_scatter | solution.py:558
  114.0 1.5 collective-permute-start
  115.7 1.9 collective-permute-done
  117.7 1.0 copy.47
  118.7 81.5 %shard_map.155 = (bf16[512,4096]{1,0:T(8,128)(2,1)}, f32[512,32]{1,0:T(8,128)S(1)}, f32[2,512,128]{2,1,0:T(8,128)S(1)}, f32[2,512,128]{2,1,0:T(8,128)S(1)}) custom-call(bf16[512,4096]{1,0:T(8,128)(2,1)} %get-tuple-element.49.x_ref, bf16[512,4096]{1,0:T(8,128)(2,1)} %get-tuple-element.48.dy_ref, f32[512,32]{1,0:T(8,128)S(1)} %copy.46.a_ref, ...), custom_call_target="tpu_custom_call" | custom-call | flops 5368709120 | bytes 16777216 | tf_op jit(solution)/shard_map/pallas_call | solution.py:570
  200.2 5.5 %copy.53 = bf16[64,8,32,128]{3,2,1,0:T(8,128)(2,1)} copy(bf16[64,8,32,128]{3,1,2,0:T(8,128)(2,1)} %bitcast.50) | data formatting | bytes 8388608
  205.7 0.7 copy.48
  206.4 1.2 copy.49
  207.6 1.2 copy.50
  208.8 6.0 %all-gather = bf16[1,512,256]{2,1,0:T(8,128)(2,1)S(1)} all-gather(bf16[1,128,256]{2,1,0:T(8,128)(2,1)} %reduce-scatter.5.cloned.1.call-done), channel_id=2, replica_groups=mesh['seq'=8,'head'=4] {'head'}, dimensions={1}, use_global_device_ids=true | all-gather | bytes 327680 | tf_op jit(solution)/shard_map/all_gather | solution.py:560
  214.8 0.7 fusion
  (23 shorter events, 0.8 us)
Async XLA Ops:
  7.2 55.6 %all-gather.3.cloned.1.call-start = ((), (), s32[]{:S(2)}) async-start(), calls=%async_computation.2 | async-start | bytes 2359296 | tf_op jit(solution)/shard_map/all_gather | solution.py:487
  8.9 104.9 %reduce-scatter.3.cloned.1.call-start = ((), (), s32[]{:S(2)}) async-start(), calls=%async_computation.3 | async-start | bytes 2621440 | tf_op jit(solution)/shard_map/reduce_scatter | solution.py:558
  16.7 13.6 %copy-start = (f32[2,512,128]{2,1,0:T(8,128)}, f32[2,512,128]{2,1,0:T(8,128)S(1)}, u32[]{:S(2)}) copy-start(f32[2,512,128]{2,1,0:T(8,128)S(1)} %get-tuple-element.50.c_ref) | copy-start | bytes 1572868
  16.7 13.6 %copy-start.1 = (f32[2,512,128]{2,1,0:T(8,128)}, f32[2,512,128]{2,1,0:T(8,128)S(1)}, u32[]{:S(2)}) copy-start(f32[2,512,128]{2,1,0:T(8,128)S(1)} %get-tuple-element.51.b_ref) | copy-start | bytes 1572868
  62.7 51.1 %copy-start.2 = (f32[512,32]{0,1:T(8,128)S(1)}, f32[512,32]{0,1:T(8,128)}, u32[]{:S(2)}) copy-start(f32[512,32]{0,1:T(8,128)} %param.11) | copy-start | bytes 196612
  83.7 125.1 %reduce-scatter.5.cloned.1.call-start = ((), (), s32[]{:S(2)}) async-start(), calls=%async_computation.4 | async-start | bytes 589824 | tf_op jit(solution)/shard_map/reduce_scatter | solution.py:559
  114.0 3.6 %collective-permute-start = (f32[1,32]{1,0:T(1,128)S(1)}, f32[1,32]{1,0:T(1,128)S(1)}, u32[]{:S(2)}, u32[]{:S(2)}) collective-permute-start(f32[1,32]{1,0:T(1,128)S(1)} %bitcast.58), channel_id=1, source_target_pairs={{0,4},{4,0},{8,12},{12,8},{16,20},{20,16},{24,28},{28,24},{1,5},{5... | collective-permute-start | bytes 392 | tf_op jit(solution)/shard_map/ppermute | solution.py:458
Sparse Core Ops, SparseCore 0:
  10.7 51.9 all-gather.2
  83.9 29.8 reduce-scatter.2
  117.5 62.9 reduce-scatter.4
